TPU v7x, 128 devices: a whole 4x4x4 slice. The times are simulated.
128 devices in a mesh: depth: 8 (over y_lo, z), strip: 16 (over x, y_hi, core).
Axes of the slice: x: 4, y: 4 (y_hi: 2, y_lo: 2; y = y_hi * 2 + y_lo), z: 4, core: 2. Of those that a mesh axis runs over, the one named last changes fastest.
Arguments:
- conductivity: float32 [128, 128, 1536], P('depth', 'strip'), may hold values from 0.3 to 3
- forward_states: float32 [5, 128, 128, 1536], P(None, 'depth', 'strip'), may hold values from -6 to 6
- sensor_cell: int32 [524288], P(('depth', 'strip')), may hold values from 0 to 196607
- sensor_window: int32 [524288], P(('depth', 'strip')), may hold values from 0 to 4
- sensor_misfit: float32 [524288], P(('depth', 'strip')), may hold values from -6 to 6
- prior_conductance: float32 [3, 32, 384, 128], P(None, 'strip', 'depth'), may hold values from 0.2 to 8, as said below
Outputs:
- coarse_grad: float32 [32, 384, 128], P('strip', 'depth')
- prior_step: float32 [32, 384, 128], P('strip', 'depth')
Inputs may be any that keep to these rules, and one draw needn't show every extreme that they name: sensor_cell indexes a cell of the block of 16 x 8 x 1536 cells of the device that holds the record. `prior_conductance`: positive conductances.
All inputs are finite; a program needn't handle non-finite values.
Results may differ from a plain program's by a relative error of at most 0.00002.
Values sent between devices are 32-bit elements; how exact they have to be, the bound alone decides.
No kernel may reach another device: no remote copies, remote signals or barrier semaphores. Data moves between devices by JAX's collectives and lax.ppermute only.
A program may use at most 128 MiB of HBM per device.

v0:
```python
import jax
import jax.numpy as jnp
from jax import lax
from jax.sharding import PartitionSpec as P

SWEEPS = 2
CHEB = 6


time_step = 1.0
matern_shift = 0.5


def with_halo(x, sides, width):
    for axis, dim in sides:
        devices, length = (lax.axis_size(axis), x.shape[dim])
        up = [(i, (i + 1) % devices) for i in range(devices - 1)]
        down = [(j, i) for i, j in up]
        last = lax.slice_in_dim(x, length - width, length, axis=dim)
        initial = lax.slice_in_dim(x, 0, width, axis=dim)
        before = lax.ppermute(last, axis, up)
        after = lax.ppermute(initial, axis, down)
        x = jnp.concatenate([before, x, after], axis=dim)
    return x


def axial(padded):
    return (
        padded[2:, 1:-1, 1:-1],
        padded[:-2, 1:-1, 1:-1],
        padded[1:-1, 2:, 1:-1],
        padded[1:-1, :-2, 1:-1],
        padded[1:-1, 1:-1, 2:],
        padded[1:-1, 1:-1, :-2],
    )


def side_pad(field):
    return jnp.pad(field, ((0, 0), (0, 0), (1, 1)))


def face_table(cond_padded):
    centre = cond_padded[1:-1, 1:-1, 1:-1]
    face_list = [0.5 * (centre + other) for other in axial(cond_padded)]
    face_total = face_list[0]
    for face in face_list[1:]:
        face_total = face_total + face
    return (face_list, 1.0 + time_step * face_total)


def relax(padded, forcing, face_list, denominator):
    beside_all = axial(padded)
    spread = face_list[0] * beside_all[0]
    for slot_index in range(1, 6):
        spread = spread + face_list[slot_index] * beside_all[slot_index]
    return (forcing + time_step * spread) / denominator


def sensitivity(adjoint, forward, adjoint_wide, forward_wide, conductivity):
    adjoint_around = axial(side_pad(adjoint_wide))
    forward_around = axial(side_pad(forward_wide))
    product = (adjoint - adjoint_around[0]) * (forward - forward_around[0])
    for slot_index in range(1, 6):
        product = product + (adjoint - adjoint_around[slot_index]) * (
            forward - forward_around[slot_index]
        )
    return -0.5 * time_step * conductivity * product


def prior_apply(vector, face_list):
    widened = with_halo(vector, (("depth", 1), ("strip", 0)), 1)
    beside_all = axial(jnp.pad(widened, ((0, 0), (0, 0), (1, 1))))
    result = matern_shift * vector
    for slot_index in range(6):
        result = result + face_list[slot_index] * (vector - beside_all[slot_index])
    return result


def on_device(
    conductivity, forward_states, sensor_cell, sensor_window, sensor_misfit, prior_conductance
):
    layers, columns, lateral = conductivity.shape
    step_count = forward_states.shape[0]
    cell_count = layers * columns * lateral
    target = sensor_window * cell_count + sensor_cell
    sources = jnp.zeros((step_count * cell_count,), jnp.float32).at[target].add(sensor_misfit)
    sources = sources.reshape(step_count, layers, columns, lateral)
    carried = jnp.zeros_like(conductivity)
    gradient = jnp.zeros_like(conductivity)
    cond_wide = with_halo(conductivity, (("depth", 0), ("strip", 1)), 1)
    face_list, denominator = face_table(side_pad(cond_wide))
    for step_index in reversed(range(step_count)):
        forcing = carried + sources[step_index]
        adjoint = forcing
        for sweep_index in range(SWEEPS):
            widened = with_halo(adjoint, (("depth", 0), ("strip", 1)), 1)
            adjoint = relax(side_pad(widened), forcing, face_list, denominator)
        stacked = jnp.stack([adjoint, forward_states[step_index]])
        both_wide = with_halo(stacked, (("depth", 1), ("strip", 2)), 1)
        gradient = gradient + sensitivity(
            adjoint, forward_states[step_index], both_wide[0], both_wide[1], conductivity
        )
        carried = adjoint
    summed = gradient.reshape(layers, columns // 4, 4, lateral // 4, 4).sum(axis=(2, 4))
    coarse_grad = lax.all_to_all(
        jnp.transpose(summed, (1, 2, 0)), "depth", split_axis=1, concat_axis=2, tiled=True
    )
    weights_wide = with_halo(prior_conductance, (("depth", 2), ("strip", 1)), 1)
    weights_wide = jnp.pad(weights_wide, ((0, 0), (0, 0), (0, 0), (1, 1)))
    prior_list = []
    for axis_index in range(3):
        beside_all = axial(weights_wide[axis_index])
        centre = weights_wide[axis_index, 1:-1, 1:-1, 1:-1]
        for side_index in range(2):
            prior_list.append(0.5 * (centre + beside_all[2 * axis_index + side_index]))
    face_total = prior_list[0]
    for face in prior_list[1:]:
        face_total = face_total + face
    upper_bound = lax.pmax(jnp.max(matern_shift + 2.0 * face_total), ("depth", "strip"))
    centre_value = 0.5 * (upper_bound + matern_shift)
    half_width = 0.5 * (upper_bound - matern_shift)
    sigma_ratio = centre_value / half_width
    recur_now = 1.0 / sigma_ratio
    solution = jnp.zeros_like(coarse_grad)
    residual = coarse_grad
    direction = residual / centre_value
    for cheb_index in range(CHEB):
        solution = solution + direction
        if cheb_index + 1 < CHEB:
            residual = residual - prior_apply(direction, prior_list)
            recur_next = 1.0 / (2.0 * sigma_ratio - recur_now)
            direction = (
                recur_next * recur_now * direction + 2.0 * recur_next / half_width * residual
            )
            recur_now = recur_next
    return (coarse_grad, solution)


def solution(mesh):
    placed = (
        P("depth", "strip", None),
        P(None, "depth", "strip", None),
        P(("depth", "strip")),
        P(("depth", "strip")),
        P(("depth", "strip")),
        P(None, "strip", "depth", None),
    )
    return jax.shard_map(
        on_device,
        mesh=mesh,
        in_specs=placed,
        out_specs=(P("strip", "depth", None), P("strip", "depth", None)),
        check_vma=False,
    )
```

profile of v0, /device:TPU:10, one launch (start us, length us, event | category | flops | bytes accessed | tf_op | source)
XLA Modules:
  0.0 604.1 jit_solution(1962387858106279581)
XLA Ops:
  1.4 24.4 %scatter_custom_fusion = f32[983040]{0:T(1024)} fusion(s32[4096]{0:T(1024)S(1)} %compare_select_fusion, f32[4096]{0:T(1024)} %param.10, f32[]{:T(128)} %constant.10.clone.1), kind=kCustom, calls=%fused_computation.8 | custom fusion | flops 4096 | bytes 3932672 | tf_op jit(solution)/shard_map/scatter-add | solution.py:86
  61.3 6.0 collective-permute-start.65
  72.3 5.9 collective-permute-start.4
  81.3 5.4 collective-permute-done.6
  96.0 6.1 %collective-permute-done.9 = f32[1,8,1536]{2,1,0:T(8,128)S(1)} collective-permute-done((f32[1,8,1536]{2,1,0:T(8,128)S(1)}, f32[1,8,1536]{2,1,0:T(8,128)S(1)}, u32[]{:S(2)}, u32[]{:S(2)}) %collective-permute-start.9) | collective-permute-done | bytes 49184 | tf_op jit(solution)/shard_map/ppermute | solution.py:21
  106.8 5.6 collective-permute-start.67
  131.2 4.9 collective-permute-start.18
  176.2 6.0 collective-permute-start.28
  184.9 5.5 collective-permute-done.29
  198.0 5.0 collective-permute-done.31
  232.7 6.0 collective-permute-start.40
  241.5 5.3 collective-permute-done.41
  289.2 6.0 collective-permute-start.52
  297.9 5.5 collective-permute-done.53
  345.3 6.0 collective-permute-start.61
  354.0 6.0 collective-permute-done.60
  368.4 5.6 collective-permute-done.62
  377.9 33.0 %fusion.11 = f32[16,8,1536]{2,1,0:T(8,128)} fusion(f32[16,8,1536]{2,1,0:T(8,128)} %get-tuple-element.32, f32[18,10,1536]{2,1,0:T(8,128)S(1)} %copy-done.3, f32[18,10,1536]{2,1,0:T(8,128)S(1)} %get-tuple-element.58, f32[16,8,1536]{2,1,0:T(8,128)} %copy-done.9, f32[18,10,1536]{2,1,0:T(8,128)} %get-tuple-element.57, f32[18,10,1536]{2,1,0:T(8,128)S(1)} %copy-done.4, ...), kind=kLoop, calls=%fused_computation.89 | loop fusion | flops 23789568 | bytes 58589184 | tf_op jit(solution)/shard_map/add | solution.py:100
  426.2 62.7 %pmax.7 = f32[]{:T(128)} all-reduce(f32[]{:T(128)} %get-tuple-element.18), channel_id=1, replica_groups=mesh['depth'=8,'strip'=16] {'depth','strip'}, use_global_device_ids=true, to_apply=%region_3.4 | all-reduce | flops 1 | bytes 8 | tf_op jit(solution)/shard_map/pmax | solution.py:119
  499.0 6.2 %collective-permute-done.68 = f32[2,1,128]{1,2,0:T(8,128)S(1)} collective-permute-done((f32[2,1,128]{1,2,0:T(8,128)S(1)}, f32[2,1,128]{1,2,0:T(8,128)S(1)}, u32[]{:S(2)}, u32[]{:S(2)}) %collective-permute-start.68) | collective-permute-done | bytes 1056 | tf_op jit(solution)/shard_map/ppermute | solution.py:21
  510.6 5.1 collective-permute-done.71
  532.3 5.5 collective-permute-done.75
  553.8 5.5 collective-permute-done.79
  575.4 5.5 collective-permute-done.83
  (347 shorter events, 360.4 us)
Async XLA Ops:
  27.2 40.2 %collective-permute-start.3 = (f32[1,8,1536]{2,1,0:T(8,128)}, f32[1,8,1536]{2,1,0:T(8,128)S(1)}, u32[]{:S(2)}, u32[]{:S(2)}) collective-permute-start(f32[1,8,1536]{2,1,0:T(8,128)} %slice.1138), channel_id=1, source_target_pairs={{0,16},{16,32},{32,48},{48,64},{64,80},{80,96},{96,112},{1,17},{17... | collective-permute-start | bytes 147464 | tf_op jit(solution)/shard_map/ppermute | solution.py:21
  31.7 35.8 %collective-permute-start.1 = (f32[1,8,1536]{2,1,0:T(8,128)}, f32[1,8,1536]{2,1,0:T(8,128)S(1)}, u32[]{:S(2)}, u32[]{:S(2)}) collective-permute-start(f32[1,8,1536]{2,1,0:T(8,128)} %slice.1133), channel_id=1, source_target_pairs={{16,0},{32,16},{48,32},{64,48},{80,64},{96,80},{112,96},{17,1},{33... | collective-permute-start | bytes 147464 | tf_op jit(solution)/shard_map/ppermute | solution.py:22
  36.4 35.6 %collective-permute-start = (f32[1,8,1536]{2,1,0:T(8,128)}, f32[1,8,1536]{2,1,0:T(8,128)S(1)}, u32[]{:S(2)}, u32[]{:S(2)}) collective-permute-start(f32[1,8,1536]{2,1,0:T(8,128)} %get-tuple-element.124), channel_id=1, source_target_pairs={{16,0},{32,16},{48,32},{64,48},{80,64},{96,80},{112,96},{17,1},{33... | collective-permute-start | bytes 147464 | tf_op jit(solution)/shard_map/ppermute | solution.py:22
  40.2 31.8 %collective-permute-start.2 = (f32[1,8,1536]{2,1,0:T(8,128)}, f32[1,8,1536]{2,1,0:T(8,128)S(1)}, u32[]{:S(2)}, u32[]{:S(2)}) collective-permute-start(f32[1,8,1536]{2,1,0:T(8,128)} %get-tuple-element.123), channel_id=1, source_target_pairs={{0,16},{16,32},{32,48},{48,64},{64,80},{80,96},{96,112},{1,17},{17... | collective-permute-start | bytes 147464 | tf_op jit(solution)/shard_map/ppermute | solution.py:21
  42.3 18.9 %collective-permute-start.64 = (f32[3,2,1,128]{3,1,2,0:T(2,128)S(1)}, f32[3,2,1,128]{3,1,2,0:T(2,128)S(1)}, u32[]{:S(2)}, u32[]{:S(2)}) collective-permute-start(f32[3,2,1,128]{3,1,2,0:T(2,128)S(1)} %copy.163), channel_id=1, source_target_pairs={{0,16},{16,32},{32,48},{48,64},{64,80},{80,96},{96,112},{1,17},{17... | collective-permute-start | bytes 9224 | tf_op jit(solution)/shard_map/ppermute | solution.py:21
  61.3 34.7 %collective-permute-start.65 = (f32[3,2,1,128]{3,1,2,0:T(2,128)S(1)}, f32[3,2,1,128]{3,1,2,0:T(2,128)S(1)}, u32[]{:S(2)}, u32[]{:S(2)}) collective-permute-start(f32[3,2,1,128]{3,1,2,0:T(2,128)S(1)} %copy.164), channel_id=1, source_target_pairs={{16,0},{32,16},{48,32},{64,48},{80,64},{96,80},{112,96},{17,1},{33... | collective-permute-start | bytes 9224 | tf_op jit(solution)/shard_map/ppermute | solution.py:22
  67.7 12.5 %collective-permute-start.5 = (f32[18,1,1536]{2,1,0:T(1,128)S(1)}, f32[18,1,1536]{2,1,0:T(1,128)S(1)}, u32[]{:S(2)}, u32[]{:S(2)}) collective-permute-start(f32[18,1,1536]{2,1,0:T(1,128)S(1)} %get-tuple-element.101), channel_id=1, source_target_pairs={{1,0},{2,1},{3,2},{4,3},{5,4},{6,5},{7,6},{8,7},{9,8},{10,9},{11,1... | collective-permute-start | bytes 331784 | tf_op jit(solution)/shard_map/ppermute | solution.py:22
  106.8 18.3 %collective-permute-start.67 = (f32[3,1,50,128]{3,1,2,0:T(1,128)S(1)}, f32[3,1,50,128]{3,1,2,0:T(1,128)S(1)}, u32[]{:S(2)}, u32[]{:S(2)}) collective-permute-start(f32[3,1,50,128]{3,1,2,0:T(1,128)S(1)} %get-tuple-element.126), channel_id=1, source_target_pairs={{1,0},{2,1},{3,2},{4,3},{5,4},{6,5},{7,6},{8,7},{9,8},{10,9},{11,1... | collective-permute-start | bytes 230408 | tf_op jit(solution)/shard_map/ppermute | solution.py:22
  112.4 12.8 %collective-permute-start.66 = (f32[3,1,50,128]{3,1,2,0:T(1,128)S(1)}, f32[3,1,50,128]{3,1,2,0:T(1,128)S(1)}, u32[]{:S(2)}, u32[]{:S(2)}) collective-permute-start(f32[3,1,50,128]{3,1,2,0:T(1,128)S(1)} %get-tuple-element.125), channel_id=1, source_target_pairs={{0,1},{1,2},{2,3},{3,4},{4,5},{5,6},{6,7},{7,8},{8,9},{9,10},{10,1... | collective-permute-start | bytes 230408 | tf_op jit(solution)/shard_map/ppermute | solution.py:21
  148.6 12.5 %collective-permute-start.20 = (f32[1,8,1536]{2,1,0:T(8,128)S(1)}, f32[1,8,1536]{2,1,0:T(8,128)S(1)}, u32[]{:S(2)}, u32[]{:S(2)}) collective-permute-start(f32[1,8,1536]{2,1,0:T(8,128)S(1)} %get-tuple-element.118), channel_id=1, source_target_pairs={{16,0},{32,16},{48,32},{64,48},{80,64},{96,80},{112,96},{17,1},{33... | collective-permute-start | bytes 147464 | tf_op jit(solution)/shard_map/ppermute | solution.py:22
  161.2 12.3 %collective-permute-start.22 = (f32[18,1,1536]{2,1,0:T(1,128)S(1)}, f32[18,1,1536]{2,1,0:T(1,128)S(1)}, u32[]{:S(2)}, u32[]{:S(2)}) collective-permute-start(f32[18,1,1536]{2,1,0:T(1,128)S(1)} %get-tuple-element.93), channel_id=1, source_target_pairs={{1,0},{2,1},{3,2},{4,3},{5,4},{6,5},{7,6},{8,7},{9,8},{10,9},{11,1... | collective-permute-start | bytes 331784 | tf_op jit(solution)/shard_map/ppermute | solution.py:22
  168.0 16.1 %collective-permute-start.15 = (f32[2,18,1,1536]{3,2,1,0:T(1,128)S(1)}, f32[2,18,1,1536]{3,2,1,0:T(1,128)S(1)}, u32[]{:S(2)}, u32[]{:S(2)}) collective-permute-start(f32[2,18,1,1536]{3,2,1,0:T(1,128)S(1)} %get-tuple-element.69), channel_id=1, source_target_pairs={{1,0},{2,1},{3,2},{4,3},{5,4},{6,5},{7,6},{8,7},{9,8},{10,9},{11,1... | collective-permute-start | bytes 663560 | tf_op jit(solution)/shard_map/ppermute | solution.py:22
  171.6 12.6 %collective-permute-start.14 = (f32[2,18,1,1536]{3,2,1,0:T(1,128)S(1)}, f32[2,18,1,1536]{3,2,1,0:T(1,128)S(1)}, u32[]{:S(2)}, u32[]{:S(2)}) collective-permute-start(f32[2,18,1,1536]{3,2,1,0:T(1,128)S(1)} %get-tuple-element.68), channel_id=1, source_target_pairs={{0,1},{1,2},{2,3},{3,4},{4,5},{5,6},{6,7},{7,8},{8,9},{9,10},{10,1... | collective-permute-start | bytes 663560 | tf_op jit(solution)/shard_map/ppermute | solution.py:21
  205.1 12.4 %collective-permute-start.32 = (f32[1,8,1536]{2,1,0:T(8,128)S(1)}, f32[1,8,1536]{2,1,0:T(8,128)S(1)}, u32[]{:S(2)}, u32[]{:S(2)}) collective-permute-start(f32[1,8,1536]{2,1,0:T(8,128)S(1)} %get-tuple-element.114), channel_id=1, source_target_pairs={{16,0},{32,16},{48,32},{64,48},{80,64},{96,80},{112,96},{17,1},{33... | collective-permute-start | bytes 147464 | tf_op jit(solution)/shard_map/ppermute | solution.py:22
  224.6 16.3 %collective-permute-start.27 = (f32[2,18,1,1536]{3,2,1,0:T(1,128)S(1)}, f32[2,18,1,1536]{3,2,1,0:T(1,128)S(1)}, u32[]{:S(2)}, u32[]{:S(2)}) collective-permute-start(f32[2,18,1,1536]{3,2,1,0:T(1,128)S(1)} %get-tuple-element.67), channel_id=1, source_target_pairs={{1,0},{2,1},{3,2},{4,3},{5,4},{6,5},{7,6},{8,7},{9,8},{10,9},{11,1... | collective-permute-start | bytes 663560 | tf_op jit(solution)/shard_map/ppermute | solution.py:22
  228.1 12.8 %collective-permute-start.26 = (f32[2,18,1,1536]{3,2,1,0:T(1,128)S(1)}, f32[2,18,1,1536]{3,2,1,0:T(1,128)S(1)}, u32[]{:S(2)}, u32[]{:S(2)}) collective-permute-start(f32[2,18,1,1536]{3,2,1,0:T(1,128)S(1)} %get-tuple-element.66), channel_id=1, source_target_pairs={{0,1},{1,2},{2,3},{3,4},{4,5},{5,6},{6,7},{7,8},{8,9},{9,10},{10,1... | collective-permute-start | bytes 663560 | tf_op jit(solution)/shard_map/ppermute | solution.py:21
  261.6 12.4 %collective-permute-start.44 = (f32[1,8,1536]{2,1,0:T(8,128)S(1)}, f32[1,8,1536]{2,1,0:T(8,128)S(1)}, u32[]{:S(2)}, u32[]{:S(2)}) collective-permute-start(f32[1,8,1536]{2,1,0:T(8,128)S(1)} %get-tuple-element.110), channel_id=1, source_target_pairs={{16,0},{32,16},{48,32},{64,48},{80,64},{96,80},{112,96},{17,1},{33... | collective-permute-start | bytes 147464 | tf_op jit(solution)/shard_map/ppermute | solution.py:22
  281.0 16.1 %collective-permute-start.39 = (f32[2,18,1,1536]{3,2,1,0:T(1,128)S(1)}, f32[2,18,1,1536]{3,2,1,0:T(1,128)S(1)}, u32[]{:S(2)}, u32[]{:S(2)}) collective-permute-start(f32[2,18,1,1536]{3,2,1,0:T(1,128)S(1)} %get-tuple-element.65), channel_id=1, source_target_pairs={{1,0},{2,1},{3,2},{4,3},{5,4},{6,5},{7,6},{8,7},{9,8},{10,9},{11,1... | collective-permute-start | bytes 663560 | tf_op jit(solution)/shard_map/ppermute | solution.py:22
  284.6 12.6 %collective-permute-start.38 = (f32[2,18,1,1536]{3,2,1,0:T(1,128)S(1)}, f32[2,18,1,1536]{3,2,1,0:T(1,128)S(1)}, u32[]{:S(2)}, u32[]{:S(2)}) collective-permute-start(f32[2,18,1,1536]{3,2,1,0:T(1,128)S(1)} %get-tuple-element.64), channel_id=1, source_target_pairs={{0,1},{1,2},{2,3},{3,4},{4,5},{5,6},{6,7},{7,8},{8,9},{9,10},{10,1... | collective-permute-start | bytes 663560 | tf_op jit(solution)/shard_map/ppermute | solution.py:21
  318.1 12.4 %collective-permute-start.56 = (f32[1,8,1536]{2,1,0:T(8,128)S(1)}, f32[1,8,1536]{2,1,0:T(8,128)S(1)}, u32[]{:S(2)}, u32[]{:S(2)}) collective-permute-start(f32[1,8,1536]{2,1,0:T(8,128)S(1)} %get-tuple-element.106), channel_id=1, source_target_pairs={{16,0},{32,16},{48,32},{64,48},{80,64},{96,80},{112,96},{17,1},{33... | collective-permute-start | bytes 147464 | tf_op jit(solution)/shard_map/ppermute | solution.py:22
  330.7 12.4 %collective-permute-start.58 = (f32[18,1,1536]{2,1,0:T(1,128)S(1)}, f32[18,1,1536]{2,1,0:T(1,128)S(1)}, u32[]{:S(2)}, u32[]{:S(2)}) collective-permute-start(f32[18,1,1536]{2,1,0:T(1,128)S(1)} %get-tuple-element.81), channel_id=1, source_target_pairs={{1,0},{2,1},{3,2},{4,3},{5,4},{6,5},{7,6},{8,7},{9,8},{10,9},{11,1... | collective-permute-start | bytes 331784 | tf_op jit(solution)/shard_map/ppermute | solution.py:22
  337.5 15.8 %collective-permute-start.51 = (f32[2,18,1,1536]{3,2,1,0:T(1,128)S(1)}, f32[2,18,1,1536]{3,2,1,0:T(1,128)S(1)}, u32[]{:S(2)}, u32[]{:S(2)}) collective-permute-start(f32[2,18,1,1536]{3,2,1,0:T(1,128)S(1)} %get-tuple-element.63), channel_id=1, source_target_pairs={{1,0},{2,1},{3,2},{4,3},{5,4},{6,5},{7,6},{8,7},{9,8},{10,9},{11,1... | collective-permute-start | bytes 663560 | tf_op jit(solution)/shard_map/ppermute | solution.py:22
  340.9 12.4 %collective-permute-start.50 = (f32[2,18,1,1536]{3,2,1,0:T(1,128)S(1)}, f32[2,18,1,1536]{3,2,1,0:T(1,128)S(1)}, u32[]{:S(2)}, u32[]{:S(2)}) collective-permute-start(f32[2,18,1,1536]{3,2,1,0:T(1,128)S(1)} %get-tuple-element.62), channel_id=1, source_target_pairs={{0,1},{1,2},{2,3},{3,4},{4,5},{5,6},{6,7},{7,8},{8,9},{9,10},{10,1... | collective-permute-start | bytes 663560 | tf_op jit(solution)/shard_map/ppermute | solution.py:21
  422.0 67.5 %all-to-all-start = ((f32[8,1,1536]{2,1,0:T(1,128)}), f32[8,1,1536]{2,1,0:T(1,128)S(1)}, u32[]{:S(2)}, u32[]{:S(2)}) async-start(f32[8,1,1536]{2,1,0:T(1,128)} %reshape.92), calls=%async_computation | async-start | bytes 98304 | tf_op jit(solution)/shard_map/all_to_all | solution.py:105
  (95 other events, 1056.7 us)
where the time goes:
time: 615 us; the launch traced here: 604 us
  starting transfers between devices  264 us (43%)
  waiting for transfers between devices  123 us (20%)
  other arithmetic  103 us (17%)
  blocking collectives  62.7 us (10%)
  local copies, waits for them, and re-layouts  45.9 us (7%)
    ppermute x44, starting transfers between devices, with_halo(): after = lax.ppermute(initial, axis, down)  154 us
    ppermute x44, waiting for transfers between devices, with_halo(): before = lax.ppermute(last, axis, up)  118 us
    ppermute x44, starting transfers between devices, with_halo(): before = lax.ppermute(last, axis, up)  107 us
    pmax x1, blocking collectives, on_device(): lax.pmax(jnp.max(matern_shift + 2.0 * face_total), ('depth', 'strip'))  62.7 us
    add x1, other arithmetic, on_device(): gradient + sensitivity(adjoint, forward_states[step_index], both_wide[0],...  33 us
    scatter-add x1, other arithmetic, on_device(): jnp.zeros((step_count * cell_count,), jnp.float32).at[target]  24.4 us
    concatenate x36, other arithmetic, with_halo(): x = jnp.concatenate([before, x, after], axis=dim)  20.4 us
  transfers between devices with their start and end apart: 89, of which 31 were waited for; matrix products, arithmetic and copies ran while one was open for 9% of the time, Pallas kernels for 0%

commit v1 on v0

v1 whole, which is shorter than its diff:
```python
import functools

import jax
import jax.numpy as jnp
from jax import lax
from jax.experimental import pallas as pl
from jax.experimental.pallas import tpu as pltpu
from jax.sharding import PartitionSpec as P

F32 = jnp.float32
STEPS = 5
CHEB = 6
CZ, CX, NY = 16, 8, 1536
TILES = NY // 128
XR = TILES * CZ
WIN = 64
SHIFT = 0.5
EXACT = lax.Precision.HIGHEST

VM = pl.BlockSpec(memory_space=pltpu.VMEM)
SM = pl.BlockSpec(memory_space=pltpu.SMEM)


def shape(*dims):
    return jax.ShapeDtypeStruct(dims, F32)


def call(body, outs, ins, scratch=(), limit=48, flops=10**7, traffic=5 * 10**6):
    return pl.pallas_call(
        body,
        out_shape=outs,
        in_specs=ins,
        out_specs=jax.tree.map(lambda _: VM, outs),
        scratch_shapes=list(scratch),
        compiler_params=pltpu.CompilerParams(vmem_limit_bytes=limit * 2**20),
        cost_estimate=pl.CostEstimate(flops=flops, bytes_accessed=traffic, transcendentals=0),
    )


def pairs_a(n):
    return [(i, i ^ 1) for i in range(n)]


def pairs_b(n):
    return [(i, (((i + 1) ^ 1) - 1) % n) for i in range(n)]


def swap(send, axis):
    n = lax.axis_size(axis)
    return lax.ppermute(send[0], axis, pairs_a(n)), lax.ppermute(send[1], axis, pairs_b(n))


def to_sides(info, k, first, second):
    odd = info[k] == 1
    below = jnp.where(info[2 + 2 * k] == 1, jnp.where(odd, first, second), 0.0)
    above = jnp.where(info[3 + 2 * k] == 1, jnp.where(odd, second, first), 0.0)
    return below, above


def from_sides(info, k, below, above):
    odd = info[k] == 1
    return jnp.where(odd, below, above), jnp.where(odd, above, below)


def iota(axis, width=NY):
    return lax.broadcasted_iota(jnp.int32, (CX, width), axis)


def lane_up(v):
    return pltpu.roll(v, NY - 1, 1)


def lane_down(v):
    return pltpu.roll(v, 1, 1)


def sub_up(v):
    return pltpu.roll(v, CX - 1, 0)


def sub_down(v):
    return pltpu.roll(v, 1, 0)


def slab_row(ref, z):
    return jnp.concatenate([ref[pl.ds(t * CZ + z, 1), :] for t in range(TILES)], axis=1)


def put_rows(info, refs, base, z, plane):
    first, second = from_sides(info, 0, plane[0:1], plane[CX - 1 : CX])
    for t in range(TILES):
        refs[0][pl.ds(base + t * CZ + z, 1), :] = first[:, t * 128 : (t + 1) * 128]
        refs[1][pl.ds(base + t * CZ + z, 1), :] = second[:, t * 128 : (t + 1) * 128]


def put_layers(info, refs, slot, low, high):
    first, second = from_sides(info, 1, low, high)
    refs[0][slot] = first
    refs[1][slot] = second


def load_sides(info, rx, base, lo_ref, hi_ref):
    lo, hi = to_sides(info, 0, rx[0][base : base + XR, :], rx[1][base : base + XR, :])
    lo_ref[...] = lo
    hi_ref[...] = hi


def load_ext(info, ref, rz, slot, ext):
    ext[1 : CZ + 1] = ref[...]
    lo, hi = to_sides(info, 1, rz[0][slot], rz[1][slot])
    ext[0] = lo
    ext[CZ + 1] = hi


EXT = pltpu.VMEM((CZ + 2, CX, NY), F32)
SIDE = pltpu.VMEM((XR, 128), F32)
FULL = (CZ, CX, NY)


def each_layer(body):
    def step(z, carry):
        body(z)
        return carry

    lax.fori_loop(0, CZ, step, 0)


def pack_forward(info, fwd, xa, xb, za, zb):
    for n in range(STEPS):
        put_layers(info, (za, zb), n, fwd[n, 0], fwd[n, CZ - 1])
        each_layer(lambda z: put_rows(info, (xa, xb), n * XR, z, fwd[n, z]))


BUFS = 4


def scatter(info, code, misfit, cond, out, xa, xb, za, zb, *parts):
    for part in parts:
        part[...] = jnp.zeros_like(part)
    place = iota(0, 128) * 128 + iota(1, 128)
    count = code.shape[0] // BUFS

    def step(i, carry):
        for k, part in enumerate(parts):
            c = code[i + k * count]
            layer = lax.shift_right_logical(c, 14)
            tile = pl.multiple_of(lax.shift_right_logical(c, 3) & (15 * 128), 128)
            add = jnp.where(place == (c & 1023), misfit[i + k * count], 0.0)
            part[layer, :, pl.ds(tile, 128)] = part[layer, :, pl.ds(tile, 128)] + add
        return carry

    lax.fori_loop(0, count, step, 0, unroll=4)

    def join(k, carry):
        total = parts[0][k]
        for part in parts[1:]:
            total = total + part[k]
        out[k // CZ, lax.rem(k, CZ)] = total
        return carry

    lax.fori_loop(0, STEPS * CZ, join, 0)
    last = STEPS - 1
    put_layers(info, (za, zb), 0, out[last, 0], out[last, CZ - 1])
    put_layers(info, (za, zb), 1, cond[0], cond[CZ - 1])

    def rows(z):
        put_rows(info, (xa, xb), 0, z, out[last, z])
        put_rows(info, (xa, xb), XR, z, cond[z])

    each_layer(rows)


def faces(info, cond, rxa, rxb, rza, rzb, fz, fy, fx, fxb, inv, ext, lo, hi):
    load_ext(info, cond, (rza, rzb), 1, ext)
    load_sides(info, (rxa, rxb), XR, lo, hi)
    sub, lane = iota(0), iota(1)

    def layer(z):
        c = ext[z + 1]
        z_lo = 0.5 * (c + ext[z])
        z_hi = 0.5 * (c + ext[z + 2])
        y_hi = 0.5 * (c + jnp.where(lane == NY - 1, 0.0, lane_up(c)))
        y_lo = jnp.where(lane == 0, 0.5 * c, lane_down(y_hi))
        x_hi = 0.5 * (c + jnp.where(sub == CX - 1, slab_row(hi, z), sub_up(c)))
        x_lo = jnp.where(sub == 0, 0.5 * (c + slab_row(lo, z)), sub_down(x_hi))
        fz[z] = z_lo
        fz[z + 1] = z_hi
        fy[z] = jnp.where(lane == NY - 1, 0.0, y_hi)
        fx[z] = jnp.where(sub == CX - 1, 0.0, x_hi)
        fxb[z] = jnp.where(sub == CX - 1, x_hi, jnp.where(sub == 0, x_lo, 0.0))
        inv[z] = 1.0 / (1.0 + (((((z_hi + z_lo) + x_hi) + x_lo) + y_hi) + y_lo))

    each_layer(layer)


def sweep(info, right, fz, fy, fx, fxb, inv, ext, lo, hi, sub, z):
    v = ext[z + 1]
    y_face = fy[z]
    x_face = fx[z]
    spread = fz[z + 1] * ext[z + 2] + fz[z] * ext[z]
    spread = spread + x_face * sub_up(v) + sub_down(x_face * v)
    spread = spread + fxb[z] * jnp.where(sub == CX - 1, slab_row(hi, z), slab_row(lo, z))
    spread = spread + y_face * lane_up(v) + lane_down(y_face * v)
    return (right[z] + spread) * inv[z]


def first_sweep(
    base, slot, info, forcing, fz, fy, fx, fxb, inv, rxa, rxb, rza, rzb, out, xa, xb, za, zb, ext, lo, hi
):
    load_ext(info, forcing, (rza, rzb), slot, ext)
    load_sides(info, (rxa, rxb), base, lo, hi)
    sub = iota(0)

    def layer(z):
        new = sweep(info, forcing, fz, fy, fx, fxb, inv, ext, lo, hi, sub, z)
        out[z] = new
        put_rows(info, (xa, xb), 0, z, new)

    each_layer(layer)
    put_layers(info, (za, zb), 0, out[0], out[CZ - 1])


def second_sweep(
    more, info, v, forcing, source, fz, fy, fx, fxb, inv, rxa, rxb, rza, rzb, out, after, xa, xb, za, zb, ext, lo, hi
):
    load_ext(info, v, (rza, rzb), 0, ext)
    load_sides(info, (rxa, rxb), 0, lo, hi)
    sub = iota(0)

    def layer(z):
        new = sweep(info, forcing, fz, fy, fx, fxb, inv, ext, lo, hi, sub, z)
        out[z] = new
        put_rows(info, (xa, xb), 0, z, new)
        if more:
            fresh = new + source[0, z]
            after[z] = fresh
            put_rows(info, (xa, xb), XR, z, fresh)

    each_layer(layer)
    put_layers(info, (za, zb), 0, out[0], out[CZ - 1])
    if more:
        put_layers(info, (za, zb), 1, after[0], after[CZ - 1])


def gradient(
    n, first, info, a_ref, f_ref, acc, rxa, rxb, rza, rzb, fxa, fxb, fza, fzb, out, a_ext, f_ext, a_lo, a_hi, f_lo, f_hi
):
    load_ext(info, a_ref, (rza, rzb), 0, a_ext)
    load_sides(info, (rxa, rxb), 0, a_lo, a_hi)
    f_ext[1 : CZ + 1] = f_ref[0]
    below, above = to_sides(info, 1, fza[n], fzb[n])
    f_ext[0] = below
    f_ext[CZ + 1] = above
    load_sides(info, (fxa, fxb), n * XR, f_lo, f_hi)
    sub, lane = iota(0), iota(1)

    def layer(z):
        a, f = a_ext[z + 1], f_ext[z + 1]
        total = (a - a_ext[z + 2]) * (f - f_ext[z + 2]) + (a - a_ext[z]) * (f - f_ext[z])
        x_hi = (a - jnp.where(sub == CX - 1, slab_row(a_hi, z), sub_up(a))) * (
            f - jnp.where(sub == CX - 1, slab_row(f_hi, z), sub_up(f))
        )
        x_lo = jnp.where(sub == 0, (a - slab_row(a_lo, z)) * (f - slab_row(f_lo, z)), sub_down(x_hi))
        y_hi = (a - jnp.where(lane == NY - 1, 0.0, lane_up(a))) * (f - jnp.where(lane == NY - 1, 0.0, lane_up(f)))
        y_lo = jnp.where(lane == 0, a * f, lane_down(y_hi))
        total = total + (x_hi + x_lo) + (y_hi + y_lo)
        out[z] = total if first else acc[z] + total

    each_layer(layer)


def coarsen(acc, cond, out, rows, tall):
    def layer(z):
        g = -0.5 * cond[z] * acc[z]
        g = g + sub_up(g)
        g = g + pltpu.roll(g, CX - 2, 0)
        rows[pl.ds(z, 1), :] = g[0:1]
        rows[pl.ds(CZ + z, 1), :] = g[4:5]

    each_layer(layer)
    group = lax.broadcasted_iota(jnp.int32, (128, 512), 1) // 4
    pick = jnp.where(group == lax.broadcasted_iota(jnp.int32, (128, 512), 0), 1.0, 0.0)
    tall[...] = jnp.zeros_like(tall)
    for k in range(3):
        tall[8 + 128 * k : 8 + 128 * (k + 1), :] = lax.dot_general(
            pick,
            rows[:, 512 * k : 512 * (k + 1)],
            (((1,), (1,)), ((), ())),
            precision=EXACT,
            preferred_element_type=F32,
        )
    for d in range(out.shape[0]):
        out[d] = tall[48 * d : 48 * d + WIN, :]


def assemble(pieces, window, coarse):
    k = lax.broadcasted_iota(jnp.int32, (2 * CZ, 128), 0)
    z = lax.broadcasted_iota(jnp.int32, (2 * CZ, 128), 1)
    for p in range(2):
        total = jnp.zeros((WIN, 128), F32)
        for d in range(pieces.shape[0]):
            own = (z >= CZ * d) & (z < CZ * (d + 1)) & (k - CZ * p == z - CZ * d)
            total = total + jnp.dot(
                pieces[d], jnp.where(own, 1.0, 0.0), precision=EXACT, preferred_element_type=F32
            )
        window[p] = total
        coarse[p] = total[8:56]


SPAN = 12


def prior_faces(first_column, first_row, w, fx, fy, fz, diag, peak):
    row = lax.broadcasted_iota(jnp.int32, (WIN, 128), 0)
    lane = lax.broadcasted_iota(jnp.int32, (WIN, 128), 1)
    y_in = (row + first_row >= 0) & (row + first_row < 384)
    y_link = y_in & (row + first_row + 1 >= 0) & (row + first_row + 1 < 384) & (row < WIN - 1)

    def x_in(j):
        return (first_column + j >= 0) & (first_column + j < 32)

    def wx(j):
        if j < 0 or j >= SPAN:
            return jnp.zeros((WIN, 128), F32)
        return jnp.where(x_in(j) & y_in, w[0, j], 0.0)

    best = None
    for j in range(SPAN):
        inside = x_in(j) & y_in
        here = wx(j)
        x_hi = 0.5 * (here + wx(j + 1))
        x_lo = 0.5 * (here + wx(j - 1))
        v = jnp.where(inside, w[1, j], 0.0)
        y_hi = 0.5 * (v + jnp.where(row == WIN - 1, 0.0, pltpu.roll(v, WIN - 1, 0)))
        y_lo = jnp.where(row == 0, 0.5 * v, pltpu.roll(y_hi, 1, 0))
        v = jnp.where(inside, w[2, j], 0.0)
        z_hi = 0.5 * (v + jnp.where(lane == 127, 0.0, pltpu.roll(v, 127, 1)))
        z_lo = jnp.where(lane == 0, 0.5 * v, pltpu.roll(z_hi, 1, 1))
        total = ((((x_hi + x_lo) + y_hi) + y_lo) + z_hi) + z_lo
        diag[j] = SHIFT + total
        fx[j] = jnp.where(inside & x_in(j + 1), x_hi, 0.0) if j + 1 < SPAN else jnp.zeros_like(x_hi)
        fy[j] = jnp.where(x_in(j) & y_link, y_hi, 0.0)
        fz[j] = jnp.where(inside & (lane < 127), z_hi, 0.0)
        if j in (5, 6):
            bound = jnp.max((SHIFT + 2.0 * total)[8:56].reshape(6, 8, 128), axis=0)
            best = bound if best is None else jnp.maximum(best, bound)
    peak[...] = best


def prior_setup(place, w, fx, fy, fz, diag, peak):
    prior_faces(place[0], place[1], w, fx, fy, fz, diag, peak)


def chebyshev(place, upper, g, fx, fy, fz, diag, out, r, d):
    row = lax.broadcasted_iota(jnp.int32, (WIN, 128), 0)
    y_in = (row + place[1] >= 0) & (row + place[1] < 384)
    top = upper[0:1, 0:1]
    centre = 0.5 * (top + SHIFT)
    half = 0.5 * (top - SHIFT)
    sigma = centre / half
    rho = 1.0 / sigma
    for j in range(SPAN):
        inside = (place[0] + j >= 0) & (place[0] + j < 32) & y_in
        start = jnp.where(inside, g[j], 0.0)
        r[j] = start
        d[0, j] = start / centre
    for p in range(2):
        out[p] = d[0, 5 + p, 8:56]
    for it in range(CHEB - 1):
        now, later = it % 2, (it + 1) % 2
        rho_new = 1.0 / (2.0 * sigma - rho)
        scale_d = rho_new * rho
        scale_r = 2.0 * rho_new / half
        for j in range(it + 1, SPAN - 1 - it):
            v = d[now, j]
            y_face, z_face = fy[j], fz[j]
            pull = fx[j] * d[now, j + 1] + fx[j - 1] * d[now, j - 1]
            pull = pull + y_face * pltpu.roll(v, WIN - 1, 0) + pltpu.roll(y_face * v, 1, 0)
            pull = pull + z_face * pltpu.roll(v, 127, 1) + pltpu.roll(z_face * v, 1, 1)
            left = r[j] - (diag[j] * v - pull)
            r[j] = left
            d[later, j] = scale_d * v + scale_r * left
        for p in range(2):
            out[p] = out[p] + d[later, 5 + p, 8:56]
        rho = rho_new


def on_device(
    conductivity, forward_states, sensor_cell, sensor_window, sensor_misfit, prior_conductance
):
    z_at, x_at = lax.axis_index("depth"), lax.axis_index("strip")
    z_n, x_n = lax.axis_size("depth"), lax.axis_size("strip")
    info = jnp.stack(
        [
            x_at % 2,
            z_at % 2,
            (x_at > 0).astype(jnp.int32),
            (x_at < x_n - 1).astype(jnp.int32),
            (z_at > 0).astype(jnp.int32),
            (z_at < z_n - 1).astype(jnp.int32),
        ]
    ).astype(jnp.int32)
    place = jnp.stack([2 * x_at - 5, 48 * z_at - 8]).astype(jnp.int32)
    x_odd, z_odd = x_at % 2 == 1, z_at % 2 == 1

    xs, zs = shape(STEPS * XR, 128), shape(STEPS, CX, NY)
    fxa, fxb, fza, fzb = call(pack_forward, (xs, xs, zs, zs), [SM, VM])(info, forward_states)
    prior_flat = prior_conductance.reshape(288, 128)
    fxa, fxb = swap((jnp.concatenate([fxa, prior_flat]), jnp.concatenate([fxb, prior_flat])), "strip")
    forward_x = (fxa, fxb)
    forward_z = swap((fza, fzb), "depth")

    layer = sensor_window * CZ + sensor_cell // (CX * NY)
    lateral = sensor_cell % NY
    code = layer * 16384 + (lateral // 128) * 1024 + (sensor_cell // NY) % CX * 128 + lateral % 128
    xs, zs = shape(2 * XR, 128), shape(2, CX, NY)
    sources, xa, xb, za, zb = call(
        scatter,
        (shape(STEPS, *FULL), xs, xs, zs, zs),
        [SM, SM, SM, VM],
        [pltpu.VMEM((STEPS * CZ, CX, NY), F32)] * BUFS,
        limit=56,
        flops=4 * 10**7,
    )(info, code, sensor_misfit, conductivity)
    rx, rz = swap((xa, xb), "strip"), swap((za, zb), "depth")

    full = shape(*FULL)
    table = call(
        faces, (shape(CZ + 1, CX, NY), full, full, full, full), [SM] + [VM] * 5, [EXT, SIDE, SIDE]
    )(info, conductivity, *rx, *rz)

    above = jnp.where(x_odd, fxb[STEPS * XR :], fxa[STEPS * XR :]).reshape(3, 2, 48, 128)
    below = jnp.where(x_odd, fxa[STEPS * XR :], fxb[STEPS * XR :]).reshape(3, 2, 48, 128)
    ring = [(i, (i + 2) % x_n) for i in range(x_n)]
    back = [(j, i) for i, j in ring]
    below2 = lax.ppermute(
        jnp.concatenate([below[:, 1:], prior_conductance], axis=1).reshape(432, 128), "strip", ring
    ).reshape(3, 3, 48, 128)
    above2 = lax.ppermute(
        jnp.concatenate([prior_conductance, above[:, :1]], axis=1).reshape(432, 128), "strip", back
    ).reshape(3, 3, 48, 128)
    weights = jnp.concatenate([below2, below, prior_conductance, above, above2], axis=1)
    low, high = weights[:, :, :8].reshape(288, 128), weights[:, :, 40:].reshape(288, 128)
    wza, wzb = swap((jnp.where(z_odd, low, high), jnp.where(z_odd, high, low)), "depth")
    under = jnp.where(z_odd, wza, wzb).reshape(3, SPAN, 8, 128)
    over = jnp.where(z_odd, wzb, wza).reshape(3, SPAN, 8, 128)
    weights = jnp.concatenate([under, weights, over], axis=2)
    span = shape(SPAN, WIN, 128)
    *prior, peak = call(prior_setup, (span, span, span, span, shape(8, 128)), [SM, VM])(place, weights)
    spread_peak = jnp.broadcast_to(jnp.max(peak), (z_n * x_n, 1, 128))
    peaks = lax.all_to_all(spread_peak, ("depth", "strip"), 0, 0)
    upper = jnp.broadcast_to(jnp.max(peaks), (8, 128))

    forcing = sources[STEPS - 1]
    base, slot = 0, 0
    acc = None
    for n in reversed(range(STEPS)):
        xs, zs = shape(XR, 128), shape(1, CX, NY)
        v, xa, xb, za, zb = call(
            functools.partial(first_sweep, base, slot),
            (full, xs, xs, zs, zs),
            [SM] + [VM] * 10,
            [EXT, SIDE, SIDE],
        )(info, forcing, *table, *rx, *rz)
        rx, rz = swap((xa, xb), "strip"), swap((za, zb), "depth")
        more = n > 0
        fields = 2 if more else 1
        xs, zs = shape(fields * XR, 128), shape(fields, CX, NY)
        before = max(n - 1, 0)
        adjoint, after, xa, xb, za, zb = call(
            functools.partial(second_sweep, more),
            (full, full if more else shape(8, 128), xs, xs, zs, zs),
            [SM] + [VM] * 12,
            [EXT, SIDE, SIDE],
        )(info, v, forcing, sources[before : before + 1], *table, *rx, *rz)
        rx, rz = swap((xa, xb), "strip"), swap((za, zb), "depth")
        first = acc is None
        acc = call(
            functools.partial(gradient, n, first),
            full,
            [SM] + [VM] * 11,
            [EXT, EXT, SIDE, SIDE, SIDE, SIDE],
        )(info, adjoint, forward_states[n : n + 1], adjoint if first else acc, *rx, *rz, *forward_x, *forward_z)
        forcing = after
        base, slot = XR, 1

    pieces = call(
        coarsen, shape(z_n, WIN, 2 * CZ), [VM, VM], [pltpu.VMEM((2 * CZ, NY), F32), pltpu.VMEM((400, 2 * CZ), F32)]
    )(acc, conductivity)
    pieces = lax.all_to_all(pieces, "depth", 0, 0)
    window, coarse_grad = call(assemble, (shape(2, WIN, 128), shape(2, 48, 128)), [VM])(pieces)
    flat = window.reshape(2 * WIN, 128)
    ga, gb = swap((flat, flat), "strip")
    above = jnp.where(x_odd, gb, ga)
    below = jnp.where(x_odd, ga, gb)
    below2 = lax.ppermute(jnp.concatenate([below[WIN:], flat]), "strip", ring)
    above2 = lax.ppermute(jnp.concatenate([flat, above[:WIN]]), "strip", back)
    g = jnp.concatenate([below2, below, flat, above, above2]).reshape(SPAN, WIN, 128)
    step = call(
        chebyshev,
        shape(2, 48, 128),
        [SM] + [VM] * 6,
        [pltpu.VMEM((SPAN, WIN, 128), F32), pltpu.VMEM((2, SPAN, WIN, 128), F32)],
    )(place, upper, g, *prior)
    return coarse_grad, step


def solution(mesh):
    placed = (
        P("depth", "strip", None),
        P(None, "depth", "strip", None),
        P(("depth", "strip")),
        P(("depth", "strip")),
        P(("depth", "strip")),
        P(None, "strip", "depth", None),
    )
    return jax.shard_map(
        on_device,
        mesh=mesh,
        in_specs=placed,
        out_specs=(P("strip", "depth", None), P("strip", "depth", None)),
        check_vma=False,
    )
```

time: 615 us -> 286 us (0.47)
  the two profiles are of different devices: /device:TPU:10 before, /device:TPU:0 now
where the time goes in v1:
time: 286 us; the launch traced here: 284 us
  Pallas kernels  90.2 us (32%)
  starting transfers between devices  77.9 us (27%)
  waiting for transfers between devices  61.3 us (21%)
  local copies, waits for them, and re-layouts  30.7 us (11%)
  blocking collectives  15.2 us (5%)
  other arithmetic  6.63 us (2%)
    ppermute x26, starting transfers between devices, swap(): lax.ppermute(send[1], axis, pairs_b(n))  64.2 us
    ppermute x26, waiting for transfers between devices, swap(): lax.ppermute(send[1], axis, pairs_b(n))  41.1 us
    unnamed x151, local copies, waits for them, and re-layouts  24.5 us
    pallas_call x5, Pallas kernels, on_device(): call(functools.partial(gradient, n, first), full, [SM] + [VM] * 11, [EXT,...  21.9 us
    pallas_call x5, Pallas kernels, on_device(): call(functools.partial(second_sweep, more), (full, full if more else shap...  20.8 us
    pallas_call x1, Pallas kernels, on_device(): call(scatter, (shape(STEPS, *FULL), xs, xs, zs, zs), [SM, SM, SM, VM], [p...  20.1 us
    pallas_call x5, Pallas kernels, on_device(): call(functools.partial(first_sweep, base, slot), (full, xs, xs, zs, zs),...  16.2 us
    all_to_all x1, blocking collectives, on_device(): peaks = lax.all_to_all(spread_peak, ('depth', 'strip'), 0, 0)  15.2 us
  transfers between devices with their start and end apart: 57, of which 21 were waited for; matrix products, arithmetic and copies ran while one was open for 4% of the time, Pallas kernels for 24%

profile of v1, /device:TPU:0, one launch (start us, length us, event | category | flops | bytes accessed | tf_op | source)
XLA Modules:
  0.0 283.7 jit_solution(4164608322695931832)
XLA Ops:
  2.7 20.1 %shard_map.77 = (f32[5,16,8,1536]{3,2,1,0:T(8,128)}, f32[384,128]{1,0:T(8,128)}, f32[384,128]{1,0:T(8,128)}, f32[2,8,1536]{2,1,0:T(8,128)}, f32[2,8,1536]{2,1,0:T(8,128)}) custom-call(s32[6]{0:T(128)} %stack.52.info, s32[4096]{0:T(1024)} %fusion.4.code, f32[4096]{0:T(1024)} %misfit.1, f32[16,8,1536]{2,1,0:T(8,128)} %cond.5), custom_call_target="tpu_custom_call" | custom-call | flops 40000000 | bytes 5000000 | tf_op jit(solution)/shard_map/pallas_call | solution.py:417
  22.8 5.6 %collective-permute-start.1 = (f32[384,128]{1,0:T(8,128)}, f32[384,128]{1,0:T(8,128)S(1)}, u32[]{:S(2)}, u32[]{:S(2)}) collective-permute-start(f32[384,128]{1,0:T(8,128)} %get-tuple-element.79), channel_id=1, source_target_pairs={{0,15},{1,2},{2,1},{3,4},{4,3},{5,6},{6,5},{7,8},{8,7},{9,10},{10,... | collective-permute-start | bytes 589832 | tf_op jit(solution)/shard_map/ppermute | solution.py:50
  50.5 4.0 %collective-permute-start.5 = (f32[192,128]{1,0:T(8,128)S(1)}, f32[192,128]{1,0:T(8,128)S(1)}, u32[]{:S(2)}, u32[]{:S(2)}) collective-permute-start(f32[192,128]{1,0:T(8,128)S(1)} %get-tuple-element.89), channel_id=1, source_target_pairs={{0,15},{1,2},{2,1},{3,4},{4,3},{5,6},{6,5},{7,8},{8,7},{9,10},{10,... | collective-permute-start | bytes 294920 | tf_op jit(solution)/shard_map/ppermute | solution.py:50
  55.5 5.1 %collective-permute-done.7.rzb = f32[1,8,1536]{2,1,0:T(8,128)S(1)} collective-permute-done((f32[1,8,1536]{2,1,0:T(8,128)S(1)}, f32[1,8,1536]{2,1,0:T(8,128)S(1)}, u32[]{:S(2)}, u32[]{:S(2)}) %collective-permute-start.7) | collective-permute-done | bytes 49184 | tf_op jit(solution)/shard_map/ppermute | solution.py:50
  60.7 3.9 %shard_map.80 = (f32[16,8,1536]{2,1,0:T(8,128)S(1)}, f32[16,8,1536]{2,1,0:T(8,128)S(1)}, f32[384,128]{1,0:T(8,128)S(1)}, f32[384,128]{1,0:T(8,128)S(1)}, f32[2,8...) custom-call(s32[6]{0:T(128)S(1)} %copy-done.59, f32[16,8,1536]{2,1,0:T(8,128)S(1)} %get-tuple-element.87.v, ...), custom_call_target="tpu_custom_call" | custom-call | flops 10000000 | bytes 5000000 | tf_op jit(solution)/shard_map/pallas_call | solution.py:470
  71.7 5.3 %collective-permute-done.11.rzb = f32[2,8,1536]{2,1,0:T(8,128)S(1)} collective-permute-done((f32[2,8,1536]{2,1,0:T(8,128)S(1)}, f32[2,8,1536]{2,1,0:T(8,128)S(1)}, u32[]{:S(2)}, u32[]{:S(2)}) %collective-permute-start.11) | collective-permute-done | bytes 98336 | tf_op jit(solution)/shard_map/ppermute | solution.py:50
  90.5 4.7 %shard_map.82 = (f32[16,8,1536]{2,1,0:T(8,128)S(1)}, f32[16,8,1536]{2,1,0:T(8,128)S(1)}, f32[384,128]{1,0:T(8,128)}, f32[384,128]{1,0:T(8,128)}, f32[2,8,1536]{2,1,0:T(8,128)S(1)}, /*index=5*/f32[2,8,1536]{2,1,0:T(8,128)}) custom-call(s32[6]{0:T(128)S(1)} %copy-done.59, f32[16,8,1536]{2,1,0:T(8,128)S(1)} %get-tuple-element.97.v, ...), custom_call_target="tpu_custom_call" | custom-call | flops 10000000 | bytes 5000000 | tf_op jit(solution)/shard_map/pallas_call | solution.py:470
  104.9 4.4 %collective-permute-done.19.rzb = f32[2,8,1536]{2,1,0:T(8,128)S(1)} collective-permute-done((f32[2,8,1536]{2,1,0:T(8,128)}, f32[2,8,1536]{2,1,0:T(8,128)S(1)}, u32[]{:S(2)}, u32[]{:S(2)}) %collective-permute-start.19) | collective-permute-done | bytes 98336 | tf_op jit(solution)/shard_map/ppermute | solution.py:50
  116.1 3.8 %collective-permute-start.21 = (f32[192,128]{1,0:T(8,128)S(1)}, f32[192,128]{1,0:T(8,128)S(1)}, u32[]{:S(2)}, u32[]{:S(2)}) collective-permute-start(f32[192,128]{1,0:T(8,128)S(1)} %get-tuple-element.109), channel_id=1, source_target_pairs={{0,15},{1,2},{2,1},{3,4},{4,3},{5,6},{6,5},{7,8},{8,7},{9,10},{10,... | collective-permute-start | bytes 294920 | tf_op jit(solution)/shard_map/ppermute | solution.py:50
  128.4 4.6 %shard_map.84 = (f32[16,8,1536]{2,1,0:T(8,128)S(1)}, f32[16,8,1536]{2,1,0:T(8,128)S(1)}, f32[384,128]{1,0:T(8,128)}, f32[384,128]{1,0:T(8,128)}, f32[2,8,1536]{2,1,0:T(8,128)S(1)}, /*index=5*/f32[2,8,1536]{2,1,0:T(8,128)S(1)}) custom-call(s32[6]{0:T(128)S(1)} %copy-done.60, f32[16,8,1536]{2,1,0:T(8,128)S(1)} %get-tuple-element.107.v, ...), custom_call_target="tpu_custom_call" | custom-call | flops 10000000 | bytes 5000000 | tf_op jit(solution)/shard_map/pallas_call | solution.py:470
  145.0 6.8 %collective-permute-done.25.rxb = f32[384,128]{1,0:T(8,128)} collective-permute-done((f32[384,128]{1,0:T(8,128)}, f32[384,128]{1,0:T(8,128)}, u32[]{:S(2)}, u32[]{:S(2)}) %collective-permute-start.25) | collective-permute-done | bytes 196640 | tf_op jit(solution)/shard_map/ppermute | solution.py:50
  171.4 4.3 %shard_map.90.acc = f32[16,8,1536]{2,1,0:T(8,128)S(1)} custom-call(s32[6]{0:T(128)S(1)} %copy-done.60, f32[16,8,1536]{2,1,0:T(8,128)S(1)} %copy-done.22, f32[1,16,8,1536]{3,2,1,0:T(8,128)S(1)} %copy-done.34, f32[16,8,1536]{2,1,0:T(8,128)S(1)} %copy-done.22, f32[384,128]{1,0:T(8,128)S(1)} %copy-done.36, f32[384,128]{1,0:T(8,128)S(1)} %copy-done.38, ...), custom_call_target="tpu_custom_call" | custom-call | flops 10000000 | bytes 5000000 | tf_op jit(solution)/shard_map/pallas_call | solution.py:478
  175.8 4.5 %shard_map.91.acc = f32[16,8,1536]{2,1,0:T(8,128)S(1)} custom-call(s32[6]{0:T(128)S(1)} %copy-done.60, f32[16,8,1536]{2,1,0:T(8,128)S(1)} %copy-done.42, f32[1,16,8,1536]{3,2,1,0:T(8,128)S(1)} %copy-done.33, f32[16,8,1536]{2,1,0:T(8,128)S(1)} %shard_map.90.acc, f32[384,128]{1,0:T(8,128)} %collective-permute-done.16.rxa, ...), custom_call_target="tpu_custom_call" | custom-call | flops 10000000 | bytes 5000000 | tf_op jit(solution)/shard_map/pallas_call | solution.py:478
  181.1 3.9 %shard_map.86 = (f32[16,8,1536]{2,1,0:T(8,128)S(1)}, f32[16,8,1536]{2,1,0:T(8,128)S(1)}, f32[384,128]{1,0:T(8,128)S(1)}, f32[384,128]{1,0:T(8,128)S(1)}, f32[2,8...) custom-call(s32[6]{0:T(128)S(1)} %copy-done.60, f32[16,8,1536]{2,1,0:T(8,128)S(1)} %copy-done.44, ...), custom_call_target="tpu_custom_call" | custom-call | flops 10000000 | bytes 5000000 | tf_op jit(solution)/shard_map/pallas_call | solution.py:470
  208.5 3.8 %shard_map.88 = (f32[16,8,1536]{2,1,0:T(8,128)S(1)}, f32[8,128]{1,0:T(8,128)}, f32[192,128]{1,0:T(8,128)S(1)}, f32[192,128]{1,0:T(8,128)S(1)}, f32[1,8,1536]{2,1,0:T(8,128)S(1)}, /*index=5*/f32[1,8,1536]{2,1,0:T(8,128)S(1)}) custom-call(s32[6]{0:T(128)S(1)} %copy-done.60, f32[16,8,1536]{2,1,0:T(8,128)S(1)} %get-tuple-element.127.v, ...), custom_call_target="tpu_custom_call" | custom-call | flops 10000000 | bytes 5000000 | tf_op jit(solution)/shard_map/pallas_call | solution.py:470
  212.3 4.2 %collective-permute-start.45 = (f32[192,128]{1,0:T(8,128)S(1)}, f32[192,128]{1,0:T(8,128)S(1)}, u32[]{:S(2)}, u32[]{:S(2)}) collective-permute-start(f32[192,128]{1,0:T(8,128)S(1)} %get-tuple-element.142), channel_id=1, source_target_pairs={{0,15},{1,2},{2,1},{3,4},{4,3},{5,6},{6,5},{7,8},{8,7},{9,10},{10,... | collective-permute-start | bytes 294920 | tf_op jit(solution)/shard_map/ppermute | solution.py:50
  217.9 4.5 %shard_map.92.acc = f32[16,8,1536]{2,1,0:T(8,128)S(1)} custom-call(s32[6]{0:T(128)S(1)} %copy-done.60, f32[16,8,1536]{2,1,0:T(8,128)S(1)} %copy-done.40, f32[1,16,8,1536]{3,2,1,0:T(8,128)S(1)} %copy-done.32, f32[16,8,1536]{2,1,0:T(8,128)S(1)} %shard_map.91.acc, f32[384,128]{1,0:T(8,128)} %collective-permute-done.24.rxa, ...), custom_call_target="tpu_custom_call" | custom-call | flops 10000000 | bytes 5000000 | tf_op jit(solution)/shard_map/pallas_call | solution.py:478
  222.4 4.3 %shard_map.93.acc = f32[16,8,1536]{2,1,0:T(8,128)S(1)} custom-call(s32[6]{0:T(128)S(1)} %copy-done.60, f32[16,8,1536]{2,1,0:T(8,128)S(1)} %get-tuple-element.133.a_ref, f32[1,16,8,1536]{3,2,1,0:T(8,128)S(1)} %copy-done.31, f32[16,8,1536]{2,1,0:T(8,128)S(1)} %shard_map.92.acc, f32[384,128]{1,0:T(8,128)S(1)} %collective-permute-done.32.rxa, ...), custom_call_target="tpu_custom_call" | custom-call | flops 10000000 | bytes 5000000 | tf_op jit(solution)/shard_map/pallas_call | solution.py:478
  226.7 4.3 %shard_map.94.acc = f32[16,8,1536]{2,1,0:T(8,128)S(1)} custom-call(s32[6]{0:T(128)S(1)} %copy-done.60, f32[16,8,1536]{2,1,0:T(8,128)S(1)} %get-tuple-element.132.a_ref, f32[1,16,8,1536]{3,2,1,0:T(8,128)S(1)} %copy-done.29, f32[16,8,1536]{2,1,0:T(8,128)S(1)} %shard_map.93.acc, f32[192,128]{1,0:T(8,128)S(1)} %collective-permute-done.44.rxa, ...), custom_call_target="tpu_custom_call" | custom-call | flops 10000000 | bytes 5000000 | tf_op jit(solution)/shard_map/pallas_call | solution.py:478
  233.1 4.3 %all-to-all-start = ((f32[8,1,2048]{2,1,0:T(1,128)}), f32[8,1,2048]{2,1,0:T(1,128)S(1)}, u32[]{:S(2)}, u32[]{:S(2)}) async-start(f32[8,1,2048]{2,1,0:T(1,128)} %reshape.58), calls=%async_computation | async-start | bytes 131072 | tf_op jit(solution)/shard_map/all_to_all | solution.py:490
  237.4 6.3 %all-to-all-done = f32[8,1,2048]{2,1,0:T(1,128)S(1)} async-done(((f32[8,1,2048]{2,1,0:T(1,128)}), f32[8,1,2048]{2,1,0:T(1,128)S(1)}, u32[]{:S(2)}, u32[]{:S(2)}) %all-to-all-start) | async-done | bytes 65568 | tf_op jit(solution)/shard_map/all_to_all | solution.py:490
  249.1 4.7 %collective-permute-done.53 = f32[128,128]{1,0:T(8,128)S(1)} collective-permute-done((f32[128,128]{1,0:T(8,128)S(1)}, f32[128,128]{1,0:T(8,128)S(1)}, u32[]{:S(2)}, u32[]{:S(2)}) %collective-permute-start.53) | collective-permute-done | bytes 65568 | tf_op jit(solution)/shard_map/ppermute | solution.py:50
  256.6 5.4 %collective-permute-done.54 = f32[192,128]{1,0:T(8,128)S(1)} collective-permute-done((f32[192,128]{1,0:T(8,128)S(1)}, f32[192,128]{1,0:T(8,128)S(1)}, u32[]{:S(2)}, u32[]{:S(2)}) %collective-permute-start.54) | collective-permute-done | bytes 98336 | tf_op jit(solution)/shard_map/ppermute | solution.py:496
  265.1 15.2 %all_to_all.10 = f32[128,1,128]{2,1,0:T(1,128)S(1)} all-to-all(f32[128,1,128]{2,1,0:T(1,128)S(1)} %broadcast_in_dim.6), channel_id=1, replica_groups=mesh['depth'=8,'strip'=16] {'depth','strip'}, dimensions={0} | all-to-all | bytes 131072 | tf_op jit(solution)/shard_map/all_to_all | solution.py:451
  (293 shorter events, 144.0 us)
Async XLA Ops:
  22.8 19.8 %collective-permute-start = (f32[384,128]{1,0:T(8,128)}, f32[384,128]{1,0:T(8,128)S(1)}, u32[]{:S(2)}, u32[]{:S(2)}) collective-permute-start(f32[384,128]{1,0:T(8,128)} %get-tuple-element.78), channel_id=1, source_target_pairs={{0,1},{1,0},{2,3},{3,2},{4,5},{5,4},{6,7},{7,6},{8,9},{9,8},{10,11... | collective-permute-start | bytes 589832 | tf_op jit(solution)/shard_map/ppermute | solution.py:50
  22.8 19.8 %collective-permute-start.1 = (f32[384,128]{1,0:T(8,128)}, f32[384,128]{1,0:T(8,128)S(1)}, u32[]{:S(2)}, u32[]{:S(2)}) collective-permute-start(f32[384,128]{1,0:T(8,128)} %get-tuple-element.79), channel_id=1, source_target_pairs={{0,15},{1,2},{2,1},{3,4},{4,3},{5,6},{6,5},{7,8},{8,7},{9,10},{10,... | collective-permute-start | bytes 589832 | tf_op jit(solution)/shard_map/ppermute | solution.py:50
  30.3 12.3 %collective-permute-start.3 = (f32[2,8,1536]{2,1,0:T(8,128)}, f32[2,8,1536]{2,1,0:T(8,128)S(1)}, u32[]{:S(2)}, u32[]{:S(2)}) collective-permute-start(f32[2,8,1536]{2,1,0:T(8,128)} %get-tuple-element.81), channel_id=1, source_target_pairs={{0,112},{16,32},{32,16},{48,64},{64,48},{80,96},{96,80},{112,0},{1... | collective-permute-start | bytes 294920 | tf_op jit(solution)/shard_map/ppermute | solution.py:50
  39.1 80.8 %collective-permute-start.40 = (f32[1248,128]{1,0:T(8,128)}, f32[1248,128]{1,0:T(8,128)}, u32[]{:S(2)}, u32[]{:S(2)}) collective-permute-start(f32[1248,128]{1,0:T(8,128)} %get-tuple-element.173), channel_id=1, source_target_pairs={{0,1},{1,0},{2,3},{3,2},{4,5},{5,4},{6,7},{7,6},{8,9},{9,8},{10,11... | collective-permute-start | bytes 1916936 | tf_op jit(solution)/shard_map/ppermute | solution.py:50
  39.2 82.8 %collective-permute-start.41 = (f32[1248,128]{1,0:T(8,128)}, f32[1248,128]{1,0:T(8,128)}, u32[]{:S(2)}, u32[]{:S(2)}) collective-permute-start(f32[1248,128]{1,0:T(8,128)} %get-tuple-element.172), channel_id=1, source_target_pairs={{0,15},{1,2},{2,1},{3,4},{4,3},{5,6},{6,5},{7,8},{8,7},{9,10},{10,... | collective-permute-start | bytes 1916936 | tf_op jit(solution)/shard_map/ppermute | solution.py:50
  65.5 11.5 %collective-permute-start.8 = (f32[384,128]{1,0:T(8,128)S(1)}, f32[384,128]{1,0:T(8,128)S(1)}, u32[]{:S(2)}, u32[]{:S(2)}) collective-permute-start(f32[384,128]{1,0:T(8,128)S(1)} %get-tuple-element.93), channel_id=1, source_target_pairs={{0,1},{1,0},{2,3},{3,2},{4,5},{5,4},{6,7},{7,6},{8,9},{9,8},{10,11... | collective-permute-start | bytes 589832 | tf_op jit(solution)/shard_map/ppermute | solution.py:50
  65.6 11.5 %collective-permute-start.9 = (f32[384,128]{1,0:T(8,128)S(1)}, f32[384,128]{1,0:T(8,128)S(1)}, u32[]{:S(2)}, u32[]{:S(2)}) collective-permute-start(f32[384,128]{1,0:T(8,128)S(1)} %get-tuple-element.94), channel_id=1, source_target_pairs={{0,15},{1,2},{2,1},{3,4},{4,3},{5,6},{6,5},{7,8},{8,7},{9,10},{10,... | collective-permute-start | bytes 589832 | tf_op jit(solution)/shard_map/ppermute | solution.py:50
  97.1 12.8 %collective-permute-start.16 = (f32[384,128]{1,0:T(8,128)}, f32[384,128]{1,0:T(8,128)}, u32[]{:S(2)}, u32[]{:S(2)}) collective-permute-start(f32[384,128]{1,0:T(8,128)} %get-tuple-element.103), channel_id=1, source_target_pairs={{0,1},{1,0},{2,3},{3,2},{4,5},{5,4},{6,7},{7,6},{8,9},{9,8},{10,11... | collective-permute-start | bytes 589832 | tf_op jit(solution)/shard_map/ppermute | solution.py:50
  97.1 12.8 %collective-permute-start.17 = (f32[384,128]{1,0:T(8,128)}, f32[384,128]{1,0:T(8,128)}, u32[]{:S(2)}, u32[]{:S(2)}) collective-permute-start(f32[384,128]{1,0:T(8,128)} %get-tuple-element.104), channel_id=1, source_target_pairs={{0,15},{1,2},{2,1},{3,4},{4,3},{5,6},{6,5},{7,8},{8,7},{9,10},{10,... | collective-permute-start | bytes 589832 | tf_op jit(solution)/shard_map/ppermute | solution.py:50
  109.9 52.5 %collective-permute-start.42 = (f32[5,8,1536]{2,1,0:T(8,128)}, f32[5,8,1536]{2,1,0:T(8,128)S(1)}, u32[]{:S(2)}, u32[]{:S(2)}) collective-permute-start(f32[5,8,1536]{2,1,0:T(8,128)} %copy-done.61), channel_id=1, source_target_pairs={{0,16},{16,0},{32,48},{48,32},{64,80},{80,64},{96,112},{112,96},{1... | collective-permute-start | bytes 737288 | tf_op jit(solution)/shard_map/ppermute | solution.py:50
  116.0 12.3 %collective-permute-start.20 = (f32[192,128]{1,0:T(8,128)S(1)}, f32[192,128]{1,0:T(8,128)S(1)}, u32[]{:S(2)}, u32[]{:S(2)}) collective-permute-start(f32[192,128]{1,0:T(8,128)S(1)} %get-tuple-element.108), channel_id=1, source_target_pairs={{0,1},{1,0},{2,3},{3,2},{4,5},{5,4},{6,7},{7,6},{8,9},{9,8},{10,11... | collective-permute-start | bytes 294920 | tf_op jit(solution)/shard_map/ppermute | solution.py:50
  116.1 12.2 %collective-permute-start.21 = (f32[192,128]{1,0:T(8,128)S(1)}, f32[192,128]{1,0:T(8,128)S(1)}, u32[]{:S(2)}, u32[]{:S(2)}) collective-permute-start(f32[192,128]{1,0:T(8,128)S(1)} %get-tuple-element.109), channel_id=1, source_target_pairs={{0,15},{1,2},{2,1},{3,4},{4,3},{5,6},{6,5},{7,8},{8,7},{9,10},{10,... | collective-permute-start | bytes 294920 | tf_op jit(solution)/shard_map/ppermute | solution.py:50
  124.0 39.1 %collective-permute-start.43 = (f32[5,8,1536]{2,1,0:T(8,128)}, f32[5,8,1536]{2,1,0:T(8,128)}, u32[]{:S(2)}, u32[]{:S(2)}) collective-permute-start(f32[5,8,1536]{2,1,0:T(8,128)} %get-tuple-element.140), channel_id=1, source_target_pairs={{0,112},{16,32},{32,16},{48,64},{64,48},{80,96},{96,80},{112,0},{1... | collective-permute-start | bytes 737288 | tf_op jit(solution)/shard_map/ppermute | solution.py:50
  136.0 52.6 %collective-permute-start.48 = (f32[432,128]{1,0:T(8,128)}, f32[432,128]{1,0:T(8,128)}, u32[]{:S(2)}, u32[]{:S(2)}) collective-permute-start(f32[432,128]{1,0:T(8,128)} %bitcast.11), channel_id=1, source_target_pairs={{0,2},{1,3},{2,4},{3,5},{4,6},{5,7},{6,8},{7,9},{8,10},{9,11},{10,... | collective-permute-start | bytes 663560 | tf_op jit(solution)/shard_map/ppermute | solution.py:436
  159.3 21.7 %collective-permute-start.28 = (f32[192,128]{1,0:T(8,128)}, f32[192,128]{1,0:T(8,128)}, u32[]{:S(2)}, u32[]{:S(2)}) collective-permute-start(f32[192,128]{1,0:T(8,128)} %get-tuple-element.118), channel_id=1, source_target_pairs={{0,1},{1,0},{2,3},{3,2},{4,5},{5,4},{6,7},{7,6},{8,9},{9,8},{10,11... | collective-permute-start | bytes 294920 | tf_op jit(solution)/shard_map/ppermute | solution.py:50
  159.3 21.7 %collective-permute-start.29 = (f32[192,128]{1,0:T(8,128)}, f32[192,128]{1,0:T(8,128)}, u32[]{:S(2)}, u32[]{:S(2)}) collective-permute-start(f32[192,128]{1,0:T(8,128)} %get-tuple-element.119), channel_id=1, source_target_pairs={{0,15},{1,2},{2,1},{3,4},{4,3},{5,6},{6,5},{7,8},{8,7},{9,10},{10,... | collective-permute-start | bytes 294920 | tf_op jit(solution)/shard_map/ppermute | solution.py:50
  162.4 17.9 %collective-permute-start.30 = (f32[1,8,1536]{2,1,0:T(8,128)}, f32[1,8,1536]{2,1,0:T(8,128)S(1)}, u32[]{:S(2)}, u32[]{:S(2)}) collective-permute-start(f32[1,8,1536]{2,1,0:T(8,128)} %get-tuple-element.120), channel_id=1, source_target_pairs={{0,16},{16,0},{32,48},{48,32},{64,80},{80,64},{96,112},{112,96},{1... | collective-permute-start | bytes 147464 | tf_op jit(solution)/shard_map/ppermute | solution.py:50
  163.1 17.9 %collective-permute-start.31 = (f32[1,8,1536]{2,1,0:T(8,128)S(1)}, f32[1,8,1536]{2,1,0:T(8,128)}, u32[]{:S(2)}, u32[]{:S(2)}) collective-permute-start(f32[1,8,1536]{2,1,0:T(8,128)S(1)} %get-tuple-element.121), channel_id=1, source_target_pairs={{0,112},{16,32},{32,16},{48,64},{64,48},{80,96},{96,80},{112,0},{1... | collective-permute-start | bytes 147464 | tf_op jit(solution)/shard_map/ppermute | solution.py:50
  180.3 57.0 %collective-permute-start.49 = (f32[432,128]{1,0:T(8,128)S(1)}, f32[432,128]{1,0:T(8,128)S(1)}, u32[]{:S(2)}, u32[]{:S(2)}) collective-permute-start(f32[432,128]{1,0:T(8,128)S(1)} %bitcast.42), channel_id=1, source_target_pairs={{2,0},{3,1},{4,2},{5,3},{6,4},{7,5},{8,6},{9,7},{10,8},{11,9},{12,... | collective-permute-start | bytes 663560 | tf_op jit(solution)/shard_map/ppermute | solution.py:439
  185.0 11.6 %collective-permute-start.32 = (f32[384,128]{1,0:T(8,128)S(1)}, f32[384,128]{1,0:T(8,128)S(1)}, u32[]{:S(2)}, u32[]{:S(2)}) collective-permute-start(f32[384,128]{1,0:T(8,128)S(1)} %get-tuple-element.123), channel_id=1, source_target_pairs={{0,1},{1,0},{2,3},{3,2},{4,5},{5,4},{6,7},{7,6},{8,9},{9,8},{10,11... | collective-permute-start | bytes 589832 | tf_op jit(solution)/shard_map/ppermute | solution.py:50
  185.1 11.5 %collective-permute-start.33 = (f32[384,128]{1,0:T(8,128)S(1)}, f32[384,128]{1,0:T(8,128)S(1)}, u32[]{:S(2)}, u32[]{:S(2)}) collective-permute-start(f32[384,128]{1,0:T(8,128)S(1)} %get-tuple-element.124), channel_id=1, source_target_pairs={{0,15},{1,2},{2,1},{3,4},{4,3},{5,6},{6,5},{7,8},{8,7},{9,10},{10,... | collective-permute-start | bytes 589832 | tf_op jit(solution)/shard_map/ppermute | solution.py:50
  212.3 14.4 %collective-permute-start.44 = (f32[192,128]{1,0:T(8,128)S(1)}, f32[192,128]{1,0:T(8,128)S(1)}, u32[]{:S(2)}, u32[]{:S(2)}) collective-permute-start(f32[192,128]{1,0:T(8,128)S(1)} %get-tuple-element.141), channel_id=1, source_target_pairs={{0,1},{1,0},{2,3},{3,2},{4,5},{5,4},{6,7},{7,6},{8,9},{9,8},{10,11... | collective-permute-start | bytes 294920 | tf_op jit(solution)/shard_map/ppermute | solution.py:50
  212.3 14.4 %collective-permute-start.45 = (f32[192,128]{1,0:T(8,128)S(1)}, f32[192,128]{1,0:T(8,128)S(1)}, u32[]{:S(2)}, u32[]{:S(2)}) collective-permute-start(f32[192,128]{1,0:T(8,128)S(1)} %get-tuple-element.142), channel_id=1, source_target_pairs={{0,15},{1,2},{2,1},{3,4},{4,3},{5,6},{6,5},{7,8},{8,7},{9,10},{10,... | collective-permute-start | bytes 294920 | tf_op jit(solution)/shard_map/ppermute | solution.py:50
  262.2 18.8 %collective-permute-start.55 = (f32[192,128]{1,0:T(8,128)S(1)}, f32[192,128]{1,0:T(8,128)S(1)}, u32[]{:S(2)}, u32[]{:S(2)}) collective-permute-start(f32[192,128]{1,0:T(8,128)S(1)} %pad_maximum_fusion.6), channel_id=1, source_target_pairs={{2,0},{3,1},{4,2},{5,3},{6,4},{7,5},{8,6},{9,7},{10,8},{11,9},{12,... | collective-permute-start | bytes 294920 | tf_op jit(solution)/shard_map/ppermute | solution.py:497
  (104 other events, 698.5 us)

commit v2 on v1

--- a/solution.py
+++ b/solution.py
@@ -25,7 +25,7 @@
     return jax.ShapeDtypeStruct(dims, F32)
 
 
-def call(body, outs, ins, scratch=(), limit=48, flops=10**7, traffic=5 * 10**6):
+def call(body, outs, ins, scratch=(), limit=6, flops=10**7, traffic=5 * 10**6):
     return pl.pallas_call(
         body,
         out_shape=outs,
@@ -103,6 +103,16 @@
     lo, hi = to_sides(info, 0, rx[0][base : base + XR, :], rx[1][base : base + XR, :])
     lo_ref[...] = lo
     hi_ref[...] = hi
+
+
+def pass_peak(mine, rx, at, sends, to, out):
+    best = mine[...]
+    if at is not None:
+        best = jnp.maximum(best, jnp.maximum(rx[0][at : at + 8, :], rx[1][at : at + 8, :]))
+    out[...] = best
+    if sends is not None:
+        for send in sends:
+            send[to : to + 8, :] = best
 
 
 def load_ext(info, ref, rz, slot, ext):
@@ -205,8 +215,10 @@
 
 
 def first_sweep(
-    base, slot, info, forcing, fz, fy, fx, fxb, inv, rxa, rxb, rza, rzb, out, xa, xb, za, zb, ext, lo, hi
+    base, slot, at, info, peak, forcing, fz, fy, fx, fxb, inv, rxa, rxb, rza, rzb,
+    out, known, xa, xb, za, zb, ext, lo, hi,
 ):
+    pass_peak(peak, (rxa, rxb), at, (xa, xb), XR, known)
     load_ext(info, forcing, (rza, rzb), slot, ext)
     load_sides(info, (rxa, rxb), base, lo, hi)
     sub = iota(0)
@@ -221,8 +233,10 @@
 
 
 def second_sweep(
-    more, info, v, forcing, source, fz, fy, fx, fxb, inv, rxa, rxb, rza, rzb, out, after, xa, xb, za, zb, ext, lo, hi
+    more, info, peak, v, forcing, source, fz, fy, fx, fxb, inv, rxa, rxb, rza, rzb,
+    out, after, known, xa, xb, za, zb, ext, lo, hi,
 ):
+    pass_peak(peak, (rxa, rxb), XR, (xa, xb), 2 * XR if more else XR, known)
     load_ext(info, v, (rza, rzb), 0, ext)
     load_sides(info, (rxa, rxb), 0, lo, hi)
     sub = iota(0)
@@ -269,7 +283,8 @@
     each_layer(layer)
 
 
-def coarsen(acc, cond, out, rows, tall):
+def coarsen(acc, cond, peak, rxa, rxb, out, known, rows, tall):
+    pass_peak(peak, (rxa, rxb), XR, None, None, known)
     def layer(z):
         g = -0.5 * cond[z] * acc[z]
         g = g + sub_up(g)
@@ -290,10 +305,15 @@
             preferred_element_type=F32,
         )
     for d in range(out.shape[0]):
-        out[d] = tall[48 * d : 48 * d + WIN, :]
-
-
-def assemble(pieces, window, coarse):
+        out[d, 0:WIN] = tall[48 * d : 48 * d + WIN, :]
+        out[d, WIN : WIN + 8] = known[:, : 2 * CZ]
+
+
+def assemble(pieces, window, coarse, upper):
+    best = pieces[0, WIN : WIN + 8]
+    for d in range(1, pieces.shape[0]):
+        best = jnp.maximum(best, pieces[d, WIN : WIN + 8])
+    upper[...] = best
     k = lax.broadcasted_iota(jnp.int32, (2 * CZ, 128), 0)
     z = lax.broadcasted_iota(jnp.int32, (2 * CZ, 128), 1)
     for p in range(2):
@@ -301,7 +321,7 @@
         for d in range(pieces.shape[0]):
             own = (z >= CZ * d) & (z < CZ * (d + 1)) & (k - CZ * p == z - CZ * d)
             total = total + jnp.dot(
-                pieces[d], jnp.where(own, 1.0, 0.0), precision=EXACT, preferred_element_type=F32
+                pieces[d, 0:WIN], jnp.where(own, 1.0, 0.0), precision=EXACT, preferred_element_type=F32
             )
         window[p] = total
         coarse[p] = total[8:56]
@@ -344,7 +364,7 @@
         if j in (5, 6):
             bound = jnp.max((SHIFT + 2.0 * total)[8:56].reshape(6, 8, 128), axis=0)
             best = bound if best is None else jnp.maximum(best, bound)
-    peak[...] = best
+    peak[...] = jnp.full((8, 128), jnp.max(best))
 
 
 def prior_setup(place, w, fx, fy, fz, diag, peak):
@@ -419,7 +439,7 @@
         (shape(STEPS, *FULL), xs, xs, zs, zs),
         [SM, SM, SM, VM],
         [pltpu.VMEM((STEPS * CZ, CX, NY), F32)] * BUFS,
-        limit=56,
+        limit=18,
         flops=4 * 10**7,
     )(info, code, sensor_misfit, conductivity)
     rx, rz = swap((xa, xb), "strip"), swap((za, zb), "depth")
@@ -447,32 +467,32 @@
     weights = jnp.concatenate([under, weights, over], axis=2)
     span = shape(SPAN, WIN, 128)
     *prior, peak = call(prior_setup, (span, span, span, span, shape(8, 128)), [SM, VM])(place, weights)
-    spread_peak = jnp.broadcast_to(jnp.max(peak), (z_n * x_n, 1, 128))
-    peaks = lax.all_to_all(spread_peak, ("depth", "strip"), 0, 0)
-    upper = jnp.broadcast_to(jnp.max(peaks), (8, 128))
-
     forcing = sources[STEPS - 1]
     base, slot = 0, 0
     acc = None
+    small = shape(8, 128)
+    known = jnp.zeros((8, 128), F32)
     for n in reversed(range(STEPS)):
-        xs, zs = shape(XR, 128), shape(1, CX, NY)
-        v, xa, xb, za, zb = call(
-            functools.partial(first_sweep, base, slot),
-            (full, xs, xs, zs, zs),
-            [SM] + [VM] * 10,
+        if n == STEPS - 2:
+            known = peak
+        xs, zs = shape(XR + 8, 128), shape(1, CX, NY)
+        v, known, xa, xb, za, zb = call(
+            functools.partial(first_sweep, base, slot, 2 * XR if n < STEPS - 1 else None),
+            (full, small, xs, xs, zs, zs),
+            [SM] + [VM] * 11,
             [EXT, SIDE, SIDE],
-        )(info, forcing, *table, *rx, *rz)
+        )(info, known, forcing, *table, *rx, *rz)
         rx, rz = swap((xa, xb), "strip"), swap((za, zb), "depth")
         more = n > 0
         fields = 2 if more else 1
-        xs, zs = shape(fields * XR, 128), shape(fields, CX, NY)
+        xs, zs = shape(fields * XR + 8, 128), shape(fields, CX, NY)
         before = max(n - 1, 0)
-        adjoint, after, xa, xb, za, zb = call(
+        adjoint, after, known, xa, xb, za, zb = call(
             functools.partial(second_sweep, more),
-            (full, full if more else shape(8, 128), xs, xs, zs, zs),
-            [SM] + [VM] * 12,
+            (full, full if more else small, small, xs, xs, zs, zs),
+            [SM] + [VM] * 13,
             [EXT, SIDE, SIDE],
-        )(info, v, forcing, sources[before : before + 1], *table, *rx, *rz)
+        )(info, known, v, forcing, sources[before : before + 1], *table, *rx, *rz)
         rx, rz = swap((xa, xb), "strip"), swap((za, zb), "depth")
         first = acc is None
         acc = call(
@@ -484,11 +504,16 @@
         forcing = after
         base, slot = XR, 1
 
-    pieces = call(
-        coarsen, shape(z_n, WIN, 2 * CZ), [VM, VM], [pltpu.VMEM((2 * CZ, NY), F32), pltpu.VMEM((400, 2 * CZ), F32)]
-    )(acc, conductivity)
+    pieces, _ = call(
+        coarsen,
+        (shape(z_n, WIN + 8, 2 * CZ), small),
+        [VM] * 5,
+        [pltpu.VMEM((2 * CZ, NY), F32), pltpu.VMEM((400, 2 * CZ), F32)],
+    )(acc, conductivity, known, *rx)
     pieces = lax.all_to_all(pieces, "depth", 0, 0)
-    window, coarse_grad = call(assemble, (shape(2, WIN, 128), shape(2, 48, 128)), [VM])(pieces)
+    window, coarse_grad, upper = call(
+        assemble, (shape(2, WIN, 128), shape(2, 48, 128), shape(8, 2 * CZ)), [VM]
+    )(pieces)
     flat = window.reshape(2 * WIN, 128)
     ga, gb = swap((flat, flat), "strip")
     above = jnp.where(x_odd, gb, ga)

time: 286 us -> 255 us (0.89)
  Pallas kernels: 90.2 us -> 70.4 us
  local copies, waits for them, and re-layouts: 30.7 us -> 23.1 us
  blocking collectives: 15.2 us -> 9.74 us
  starting transfers between devices: 77.9 us -> 81.5 us
  waiting for transfers between devices: 61.3 us -> 64.4 us
    ppermute x26, waiting for transfers between devices: 41.1 us -> 23.1 us  [swap(): lax.ppermute(send[1], axis, pairs_b(n))]
    ppermute x26, waiting for transfers between devices: 8.5 us -> 25.4 us  [swap(): lax.ppermute(send[0], axis, pairs_a(n))]
    pallas_call x12, Pallas kernels: 39.3 us -> 27.2 us  [the longest x5 13 us: on_device(): call(functools.partial(second_sweep, more), (full, full if more else smal...]
    ppermute x1, starting transfers between devices: 0.66 us -> 7.53 us  [on_device(): lax.ppermute(jnp.concatenate([prior_conductance, above[:, :1]], axis=1).r...]
    all_to_all x1 -> x0, waiting for transfers between devices: 6.32 us -> none  [on_device(): pieces = lax.all_to_all(pieces, 'depth', 0, 0)]
    unnamed x151 -> x113, local copies, waits for them, and re-layouts: 24.5 us -> 18.3 us
    ppermute x1, waiting for transfers between devices: 0.01 us -> 6.11 us  [on_device(): above2 = lax.ppermute(jnp.concatenate([flat, above[:WIN]]), 'strip', back)]
    all_to_all x1, blocking collectives: 15.2 us -> 9.74 us  [on_device(): pieces = lax.all_to_all(pieces, 'depth', 0, 0)]
  transfers between devices with their start and end apart: 57 -> 56, of which waited for: 21 -> 19; matrix products, arithmetic and copies ran while one was open for 4% -> 3% of each run, Pallas kernels for 24% -> 18%
where the time goes in v2:
time: 255 us
  starting transfers between devices  81.5 us (32%)
  Pallas kernels  70.4 us (28%)
  waiting for transfers between devices  64.4 us (25%)
  local copies, waits for them, and re-layouts  23.1 us (9%)
  blocking collectives  9.74 us (4%)
  other arithmetic  3.97 us (2%)
    ppermute x26, starting transfers between devices, swap(): lax.ppermute(send[1], axis, pairs_b(n))  62.3 us
    ppermute x26, waiting for transfers between devices, swap(): lax.ppermute(send[0], axis, pairs_a(n))  25.4 us
    ppermute x26, waiting for transfers between devices, swap(): lax.ppermute(send[1], axis, pairs_b(n))  23.1 us
    unnamed x113, local copies, waits for them, and re-layouts  18.3 us
    pallas_call x1, Pallas kernels, on_device(): call(scatter, (shape(STEPS, *FULL), xs, xs, zs, zs), [SM, SM, SM, VM], [p...  17.7 us
    pallas_call x5, Pallas kernels, on_device(): call(functools.partial(gradient, n, first), full, [SM] + [VM] * 11, [EXT,...  17.2 us
    pallas_call x5, Pallas kernels, on_device(): call(functools.partial(second_sweep, more), (full, full if more else smal...  13 us
    pallas_call x5, Pallas kernels, on_device(): call(functools.partial(first_sweep, base, slot, 2 * XR if n < STEPS - 1 e...  11.9 us
  transfers between devices with their start and end apart: 56, of which 19 were waited for; matrix products, arithmetic and copies ran while one was open for 3% of the time, Pallas kernels for 18%

profile of v2, /device:TPU:0, one launch (start us, length us, event | category | flops | bytes accessed | tf_op | source)
XLA Modules:
  0.0 254.6 jit_solution(9567686992054296617)
XLA Ops:
  6.8 4.9 %collective-permute-start.1 = (f32[1248,128]{1,0:T(8,128)}, f32[1248,128]{1,0:T(8,128)S(1)}, u32[]{:S(2)}, u32[]{:S(2)}) collective-permute-start(f32[1248,128]{1,0:T(8,128)} %get-tuple-element.195), channel_id=1, source_target_pairs={{0,15},{1,2},{2,1},{3,4},{4,3},{5,6},{6,5},{7,8},{8,7},{9,10},{10,... | collective-permute-start | bytes 1916936 | tf_op jit(solution)/shard_map/ppermute | solution.py:50
  11.8 17.7 %shard_map.79 = (f32[5,16,8,1536]{3,2,1,0:T(8,128)S(1)}, f32[384,128]{1,0:T(8,128)S(1)}, f32[384,128]{1,0:T(8,128)S(1)}, f32[2,8,1536]{2,1,0:T(8,128)S(1)}, f32[2,8,1536]{2,1,0:T(8,128)S(1)}) custom-call(s32[6]{0:T(128)S(1)} %stack.52.info, s32[4096]{0:T(1024)S(1)} %fusion.4.code, f32[4096]{0:T(1024)S(1)} %copy-done.35, f32[16,8,1536]{2,1,0:T(8,128)S(1)} %copy-done.9), custom_call_target="tpu_custom_call" | custom-call | flops 40000000 | bytes 5000000 | tf_op jit(solution)/shard_map/pallas_call | solution.py:437
  34.5 3.5 %collective-permute-start.9 = (f32[2,8,1536]{2,1,0:T(8,128)S(1)}, f32[2,8,1536]{2,1,0:T(8,128)S(1)}, u32[]{:S(2)}, u32[]{:S(2)}) collective-permute-start(f32[2,8,1536]{2,1,0:T(8,128)S(1)} %get-tuple-element.95), channel_id=1, source_target_pairs={{0,112},{16,32},{32,16},{48,64},{64,48},{80,96},{96,80},{112,0},{1... | collective-permute-start | bytes 294920 | tf_op jit(solution)/shard_map/ppermute | solution.py:50
  41.3 4.0 %fusion.14 = (f32[1,16,8,1536]{3,2,1,0:T(8,128)}, f32[1,16,8,1536]{3,2,1,0:T(8,128)}, f32[1,16,8,1536]{3,2,1,0:T(8,128)}, f32[1,16,8,1536]{3,2,1,0:T(8,128)}, f32[16,8,1536]{2,1,0:T(8,128)}) fusion(f32[5,16,8,1536]{3,2,1,0:T(8,128)} %copy-done.15), kind=kLoop, calls=%fused_computation.56 | loop fusion | bytes 7864320 | tf_op jit(solution)/shard_map/slice | solution.py:495
  58.3 7.5 %collective-permute-start.3 = (f32[432,128]{1,0:T(8,128)S(1)}, f32[432,128]{1,0:T(8,128)S(1)}, u32[]{:S(2)}, u32[]{:S(2)}) collective-permute-start(f32[432,128]{1,0:T(8,128)S(1)} %bitcast.36), channel_id=1, source_target_pairs={{2,0},{3,1},{4,2},{5,3},{6,4},{7,5},{8,6},{9,7},{10,8},{11,9},{12,... | collective-permute-start | bytes 663560 | tf_op jit(solution)/shard_map/ppermute | solution.py:459
  73.3 6.8 %collective-permute-start.11 = (f32[200,128]{1,0:T(8,128)}, f32[200,128]{1,0:T(8,128)S(1)}, u32[]{:S(2)}, u32[]{:S(2)}) collective-permute-start(f32[200,128]{1,0:T(8,128)} %copy-done.40), channel_id=1, source_target_pairs={{0,15},{1,2},{2,1},{3,4},{4,3},{5,6},{6,5},{7,8},{8,7},{9,10},{10,... | collective-permute-start | bytes 307208 | tf_op jit(solution)/shard_map/ppermute | solution.py:50
  82.1 4.3 %collective-permute-done.13.rzb = f32[1,8,1536]{2,1,0:T(8,128)S(1)} collective-permute-done((f32[1,8,1536]{2,1,0:T(8,128)S(1)}, f32[1,8,1536]{2,1,0:T(8,128)S(1)}, u32[]{:S(2)}, u32[]{:S(2)}) %collective-permute-start.13) | collective-permute-done | bytes 49184 | tf_op jit(solution)/shard_map/ppermute | solution.py:50
  106.5 3.4 %collective-permute-start.19 = (f32[200,128]{1,0:T(8,128)S(1)}, f32[200,128]{1,0:T(8,128)S(1)}, u32[]{:S(2)}, u32[]{:S(2)}) collective-permute-start(f32[200,128]{1,0:T(8,128)S(1)} %get-tuple-element.115), channel_id=1, source_target_pairs={{0,15},{1,2},{2,1},{3,4},{4,3},{5,6},{6,5},{7,8},{8,7},{9,10},{10,... | collective-permute-start | bytes 307208 | tf_op jit(solution)/shard_map/ppermute | solution.py:50
  110.0 4.1 %collective-permute-done.20.rza = f32[1,8,1536]{2,1,0:T(8,128)S(1)} collective-permute-done((f32[1,8,1536]{2,1,0:T(8,128)S(1)}, f32[1,8,1536]{2,1,0:T(8,128)S(1)}, u32[]{:S(2)}, u32[]{:S(2)}) %collective-permute-start.20) | collective-permute-done | bytes 49184 | tf_op jit(solution)/shard_map/ppermute | solution.py:50
  122.1 3.4 %collective-permute-done.24.rza = f32[2,8,1536]{2,1,0:T(8,128)S(1)} collective-permute-done((f32[2,8,1536]{2,1,0:T(8,128)S(1)}, f32[2,8,1536]{2,1,0:T(8,128)S(1)}, u32[]{:S(2)}, u32[]{:S(2)}) %collective-permute-start.24) | collective-permute-done | bytes 98336 | tf_op jit(solution)/shard_map/ppermute | solution.py:50
  147.2 3.4 %collective-permute-done.32.rza = f32[2,8,1536]{2,1,0:T(8,128)S(1)} collective-permute-done((f32[2,8,1536]{2,1,0:T(8,128)S(1)}, f32[2,8,1536]{2,1,0:T(8,128)S(1)}, u32[]{:S(2)}, u32[]{:S(2)}) %collective-permute-start.32) | collective-permute-done | bytes 98336 | tf_op jit(solution)/shard_map/ppermute | solution.py:50
  156.1 5.1 %collective-permute-start.35 = (f32[200,128]{1,0:T(8,128)S(1)}, f32[200,128]{1,0:T(8,128)S(1)}, u32[]{:S(2)}, u32[]{:S(2)}) collective-permute-start(f32[200,128]{1,0:T(8,128)S(1)} %get-tuple-element.139), channel_id=1, source_target_pairs={{0,15},{1,2},{2,1},{3,4},{4,3},{5,6},{6,5},{7,8},{8,7},{9,10},{10,... | collective-permute-start | bytes 307208 | tf_op jit(solution)/shard_map/ppermute | solution.py:50
  161.6 3.6 %collective-permute-done.36.rza = f32[1,8,1536]{2,1,0:T(8,128)S(1)} collective-permute-done((f32[1,8,1536]{2,1,0:T(8,128)S(1)}, f32[1,8,1536]{2,1,0:T(8,128)S(1)}, u32[]{:S(2)}, u32[]{:S(2)}) %collective-permute-start.36) | collective-permute-done | bytes 49184 | tf_op jit(solution)/shard_map/ppermute | solution.py:50
  174.0 6.6 %collective-permute-done.40.rza = f32[2,8,1536]{2,1,0:T(8,128)S(1)} collective-permute-done((f32[2,8,1536]{2,1,0:T(8,128)S(1)}, f32[2,8,1536]{2,1,0:T(8,128)S(1)}, u32[]{:S(2)}, u32[]{:S(2)}) %collective-permute-start.40) | collective-permute-done | bytes 98336 | tf_op jit(solution)/shard_map/ppermute | solution.py:50
  182.9 4.8 %collective-permute-start.43 = (f32[200,128]{1,0:T(8,128)S(1)}, f32[200,128]{1,0:T(8,128)S(1)}, u32[]{:S(2)}, u32[]{:S(2)}) collective-permute-start(f32[200,128]{1,0:T(8,128)S(1)} %get-tuple-element.151), channel_id=1, source_target_pairs={{0,15},{1,2},{2,1},{3,4},{4,3},{5,6},{6,5},{7,8},{8,7},{9,10},{10,... | collective-permute-start | bytes 307208 | tf_op jit(solution)/shard_map/ppermute | solution.py:50
  201.0 3.4 %shard_map.91.acc = f32[16,8,1536]{2,1,0:T(8,128)S(1)} custom-call(s32[6]{0:T(128)S(1)} %stack.52.info, f32[16,8,1536]{2,1,0:T(8,128)S(1)} %get-tuple-element.158.a_ref.acc, f32[1,16,8,1536]{3,2,1,0:T(8,128)S(1)} %get-tuple-element.176.f_ref, f32[16,8,1536]{2,1,0:T(8,128)S(1)} %get-tuple-element.158.a_ref.acc, f32[392,128]{1,0:T(8,128)S(1)} %collective-permute-done.14.rxa, ...), custom_call_target="tpu_custom_call" | custom-call | flops 10000000 | bytes 5000000 | tf_op jit(solution)/shard_map/pallas_call | solution.py:498
  204.4 3.5 %shard_map.92.acc = f32[16,8,1536]{2,1,0:T(8,128)S(1)} custom-call(s32[6]{0:T(128)S(1)} %stack.52.info, f32[16,8,1536]{2,1,0:T(8,128)S(1)} %get-tuple-element.157.a_ref, f32[1,16,8,1536]{3,2,1,0:T(8,128)S(1)} %get-tuple-element.180.f_ref, f32[16,8,1536]{2,1,0:T(8,128)S(1)} %shard_map.91.acc, f32[392,128]{1,0:T(8,128)S(1)} %collective-permute-done.22.rxa, ...), custom_call_target="tpu_custom_call" | custom-call | flops 10000000 | bytes 5000000 | tf_op jit(solution)/shard_map/pallas_call | solution.py:498
  207.8 3.5 %shard_map.93.acc = f32[16,8,1536]{2,1,0:T(8,128)S(1)} custom-call(s32[6]{0:T(128)S(1)} %stack.52.info, f32[16,8,1536]{2,1,0:T(8,128)S(1)} %get-tuple-element.156.a_ref, f32[1,16,8,1536]{3,2,1,0:T(8,128)S(1)} %get-tuple-element.177.f_ref, f32[16,8,1536]{2,1,0:T(8,128)S(1)} %shard_map.92.acc, f32[392,128]{1,0:T(8,128)S(1)} %collective-permute-done.30.rxa, ...), custom_call_target="tpu_custom_call" | custom-call | flops 10000000 | bytes 5000000 | tf_op jit(solution)/shard_map/pallas_call | solution.py:498
  211.3 3.5 %shard_map.94.acc = f32[16,8,1536]{2,1,0:T(8,128)S(1)} custom-call(s32[6]{0:T(128)S(1)} %stack.52.info, f32[16,8,1536]{2,1,0:T(8,128)S(1)} %get-tuple-element.155.a_ref, f32[1,16,8,1536]{3,2,1,0:T(8,128)S(1)} %get-tuple-element.178.f_ref, f32[16,8,1536]{2,1,0:T(8,128)S(1)} %shard_map.93.acc, f32[392,128]{1,0:T(8,128)S(1)} %collective-permute-done.38.rxa, ...), custom_call_target="tpu_custom_call" | custom-call | flops 10000000 | bytes 5000000 | tf_op jit(solution)/shard_map/pallas_call | solution.py:498
  214.8 3.5 %shard_map.95.acc = f32[16,8,1536]{2,1,0:T(8,128)S(1)} custom-call(s32[6]{0:T(128)S(1)} %stack.52.info, f32[16,8,1536]{2,1,0:T(8,128)S(1)} %get-tuple-element.154.a_ref, f32[1,16,8,1536]{3,2,1,0:T(8,128)S(1)} %get-tuple-element.179.f_ref, f32[16,8,1536]{2,1,0:T(8,128)S(1)} %shard_map.94.acc, f32[200,128]{1,0:T(8,128)S(1)} %collective-permute-done.48.rxa, ...), custom_call_target="tpu_custom_call" | custom-call | flops 10000000 | bytes 5000000 | tf_op jit(solution)/shard_map/pallas_call | solution.py:498
  219.6 9.7 %all_to_all.5 = f32[8,72,32]{1,2,0:T(8,128)S(1)} all-to-all(f32[8,72,32]{1,2,0:T(8,128)S(1)} %copy.8), channel_id=1, replica_groups=mesh['depth'=8,'strip'=16] {'depth'}, dimensions={0} | all-to-all | bytes 147456 | tf_op jit(solution)/shard_map/all_to_all | solution.py:513
  230.6 4.2 %collective-permute-start.53 = (f32[128,128]{1,0:T(8,128)S(1)}, f32[128,128]{1,0:T(8,128)S(1)}, u32[]{:S(2)}, u32[]{:S(2)}) collective-permute-start(f32[128,128]{1,0:T(8,128)S(1)} %bitcast.25), channel_id=1, source_target_pairs={{0,15},{1,2},{2,1},{3,4},{4,3},{5,6},{6,5},{7,8},{8,7},{9,10},{10,... | collective-permute-start | bytes 196616 | tf_op jit(solution)/shard_map/ppermute | solution.py:50
  238.9 7.4 %collective-permute-done.54 = f32[192,128]{1,0:T(8,128)S(1)} collective-permute-done((f32[192,128]{1,0:T(8,128)S(1)}, f32[192,128]{1,0:T(8,128)S(1)}, u32[]{:S(2)}, u32[]{:S(2)}) %collective-permute-start.54) | collective-permute-done | bytes 98336 | tf_op jit(solution)/shard_map/ppermute | solution.py:521
  246.5 6.1 %collective-permute-done.55 = f32[192,128]{1,0:T(8,128)S(1)} collective-permute-done((f32[192,128]{1,0:T(8,128)S(1)}, f32[192,128]{1,0:T(8,128)S(1)}, u32[]{:S(2)}, u32[]{:S(2)}) %collective-permute-start.55) | collective-permute-done | bytes 98336 | tf_op jit(solution)/shard_map/ppermute | solution.py:522
  (248 shorter events, 125.3 us)
Async XLA Ops:
  6.8 27.6 %collective-permute-start.1 = (f32[1248,128]{1,0:T(8,128)}, f32[1248,128]{1,0:T(8,128)S(1)}, u32[]{:S(2)}, u32[]{:S(2)}) collective-permute-start(f32[1248,128]{1,0:T(8,128)} %get-tuple-element.195), channel_id=1, source_target_pairs={{0,15},{1,2},{2,1},{3,4},{4,3},{5,6},{6,5},{7,8},{8,7},{9,10},{10,... | collective-permute-start | bytes 1916936 | tf_op jit(solution)/shard_map/ppermute | solution.py:50
  11.8 26.3 %collective-permute-start = (f32[1248,128]{1,0:T(8,128)S(1)}, f32[1248,128]{1,0:T(8,128)S(1)}, u32[]{:S(2)}, u32[]{:S(2)}) collective-permute-start(f32[1248,128]{1,0:T(8,128)S(1)} %get-tuple-element.194), channel_id=1, source_target_pairs={{0,1},{1,0},{2,3},{3,2},{4,5},{5,4},{6,7},{7,6},{8,9},{9,8},{10,11... | collective-permute-start | bytes 1916936 | tf_op jit(solution)/shard_map/ppermute | solution.py:50
  31.5 14.5 %collective-permute-start.6 = (f32[384,128]{1,0:T(8,128)S(1)}, f32[384,128]{1,0:T(8,128)S(1)}, u32[]{:S(2)}, u32[]{:S(2)}) collective-permute-start(f32[384,128]{1,0:T(8,128)S(1)} %get-tuple-element.92), channel_id=1, source_target_pairs={{0,1},{1,0},{2,3},{3,2},{4,5},{5,4},{6,7},{7,6},{8,9},{9,8},{10,11... | collective-permute-start | bytes 589832 | tf_op jit(solution)/shard_map/ppermute | solution.py:50
  32.0 14.0 %collective-permute-start.7 = (f32[384,128]{1,0:T(8,128)S(1)}, f32[384,128]{1,0:T(8,128)S(1)}, u32[]{:S(2)}, u32[]{:S(2)}) collective-permute-start(f32[384,128]{1,0:T(8,128)S(1)} %get-tuple-element.93), channel_id=1, source_target_pairs={{0,15},{1,2},{2,1},{3,4},{4,3},{5,6},{6,5},{7,8},{8,7},{9,10},{10,... | collective-permute-start | bytes 589832 | tf_op jit(solution)/shard_map/ppermute | solution.py:50
  32.5 12.9 %collective-permute-start.8 = (f32[2,8,1536]{2,1,0:T(8,128)S(1)}, f32[2,8,1536]{2,1,0:T(8,128)S(1)}, u32[]{:S(2)}, u32[]{:S(2)}) collective-permute-start(f32[2,8,1536]{2,1,0:T(8,128)S(1)} %get-tuple-element.94), channel_id=1, source_target_pairs={{0,16},{16,0},{32,48},{48,32},{64,80},{80,64},{96,112},{112,96},{1... | collective-permute-start | bytes 294920 | tf_op jit(solution)/shard_map/ppermute | solution.py:50
  34.5 10.9 %collective-permute-start.9 = (f32[2,8,1536]{2,1,0:T(8,128)S(1)}, f32[2,8,1536]{2,1,0:T(8,128)S(1)}, u32[]{:S(2)}, u32[]{:S(2)}) collective-permute-start(f32[2,8,1536]{2,1,0:T(8,128)S(1)} %get-tuple-element.95), channel_id=1, source_target_pairs={{0,112},{16,32},{32,16},{48,64},{64,48},{80,96},{96,80},{112,0},{1... | collective-permute-start | bytes 294920 | tf_op jit(solution)/shard_map/ppermute | solution.py:50
  39.0 26.8 %collective-permute-start.2 = (f32[432,128]{1,0:T(8,128)}, f32[432,128]{1,0:T(8,128)}, u32[]{:S(2)}, u32[]{:S(2)}) collective-permute-start(f32[432,128]{1,0:T(8,128)} %bitcast.10), channel_id=1, source_target_pairs={{0,2},{1,3},{2,4},{3,5},{4,6},{5,7},{6,8},{7,9},{8,10},{9,11},{10,... | collective-permute-start | bytes 663560 | tf_op jit(solution)/shard_map/ppermute | solution.py:456
  58.0 22.1 %collective-permute-start.12 = (f32[1,8,1536]{2,1,0:T(8,128)}, f32[1,8,1536]{2,1,0:T(8,128)S(1)}, u32[]{:S(2)}, u32[]{:S(2)}) collective-permute-start(f32[1,8,1536]{2,1,0:T(8,128)} %get-tuple-element.105), channel_id=1, source_target_pairs={{0,16},{16,0},{32,48},{48,32},{64,80},{80,64},{96,112},{112,96},{1... | collective-permute-start | bytes 147464 | tf_op jit(solution)/shard_map/ppermute | solution.py:50
  58.3 11.0 %collective-permute-start.3 = (f32[432,128]{1,0:T(8,128)S(1)}, f32[432,128]{1,0:T(8,128)S(1)}, u32[]{:S(2)}, u32[]{:S(2)}) collective-permute-start(f32[432,128]{1,0:T(8,128)S(1)} %bitcast.36), channel_id=1, source_target_pairs={{2,0},{3,1},{4,2},{5,3},{6,4},{7,5},{8,6},{9,7},{10,8},{11,9},{12,... | collective-permute-start | bytes 663560 | tf_op jit(solution)/shard_map/ppermute | solution.py:459
  70.3 25.3 %collective-permute-start.4 = (f32[288,128]{1,0:T(8,128)}, f32[288,128]{1,0:T(8,128)}, u32[]{:S(2)}, u32[]{:S(2)}) collective-permute-start(f32[288,128]{1,0:T(8,128)} %bitcast.15), channel_id=1, source_target_pairs={{0,16},{16,0},{32,48},{48,32},{64,80},{80,64},{96,112},{112,96},{1... | collective-permute-start | bytes 442376 | tf_op jit(solution)/shard_map/ppermute | solution.py:50
  72.2 25.2 %collective-permute-start.5 = (f32[288,128]{1,0:T(8,128)}, f32[288,128]{1,0:T(8,128)}, u32[]{:S(2)}, u32[]{:S(2)}) collective-permute-start(f32[288,128]{1,0:T(8,128)} %bitcast.16), channel_id=1, source_target_pairs={{0,112},{16,32},{32,16},{48,64},{64,48},{80,96},{96,80},{112,0},{1... | collective-permute-start | bytes 442376 | tf_op jit(solution)/shard_map/ppermute | solution.py:50
  73.3 13.0 %collective-permute-start.10 = (f32[200,128]{1,0:T(8,128)}, f32[200,128]{1,0:T(8,128)S(1)}, u32[]{:S(2)}, u32[]{:S(2)}) collective-permute-start(f32[200,128]{1,0:T(8,128)} %copy-done.41), channel_id=1, source_target_pairs={{0,1},{1,0},{2,3},{3,2},{4,5},{5,4},{6,7},{7,6},{8,9},{9,8},{10,11... | collective-permute-start | bytes 307208 | tf_op jit(solution)/shard_map/ppermute | solution.py:50
  73.3 13.0 %collective-permute-start.11 = (f32[200,128]{1,0:T(8,128)}, f32[200,128]{1,0:T(8,128)S(1)}, u32[]{:S(2)}, u32[]{:S(2)}) collective-permute-start(f32[200,128]{1,0:T(8,128)} %copy-done.40), channel_id=1, source_target_pairs={{0,15},{1,2},{2,1},{3,4},{4,3},{5,6},{6,5},{7,8},{8,7},{9,10},{10,... | collective-permute-start | bytes 307208 | tf_op jit(solution)/shard_map/ppermute | solution.py:50
  156.0 11.4 %collective-permute-start.34 = (f32[200,128]{1,0:T(8,128)S(1)}, f32[200,128]{1,0:T(8,128)S(1)}, u32[]{:S(2)}, u32[]{:S(2)}) collective-permute-start(f32[200,128]{1,0:T(8,128)S(1)} %get-tuple-element.138), channel_id=1, source_target_pairs={{0,1},{1,0},{2,3},{3,2},{4,5},{5,4},{6,7},{7,6},{8,9},{9,8},{10,11... | collective-permute-start | bytes 307208 | tf_op jit(solution)/shard_map/ppermute | solution.py:50
  156.1 11.3 %collective-permute-start.35 = (f32[200,128]{1,0:T(8,128)S(1)}, f32[200,128]{1,0:T(8,128)S(1)}, u32[]{:S(2)}, u32[]{:S(2)}) collective-permute-start(f32[200,128]{1,0:T(8,128)S(1)} %get-tuple-element.139), channel_id=1, source_target_pairs={{0,15},{1,2},{2,1},{3,4},{4,3},{5,6},{6,5},{7,8},{8,7},{9,10},{10,... | collective-permute-start | bytes 307208 | tf_op jit(solution)/shard_map/ppermute | solution.py:50
  169.8 10.8 %collective-permute-start.38 = (f32[392,128]{1,0:T(8,128)S(1)}, f32[392,128]{1,0:T(8,128)S(1)}, u32[]{:S(2)}, u32[]{:S(2)}) collective-permute-start(f32[392,128]{1,0:T(8,128)S(1)} %get-tuple-element.144), channel_id=1, source_target_pairs={{0,1},{1,0},{2,3},{3,2},{4,5},{5,4},{6,7},{7,6},{8,9},{9,8},{10,11... | collective-permute-start | bytes 602120 | tf_op jit(solution)/shard_map/ppermute | solution.py:50
  169.9 10.7 %collective-permute-start.39 = (f32[392,128]{1,0:T(8,128)S(1)}, f32[392,128]{1,0:T(8,128)S(1)}, u32[]{:S(2)}, u32[]{:S(2)}) collective-permute-start(f32[392,128]{1,0:T(8,128)S(1)} %get-tuple-element.145), channel_id=1, source_target_pairs={{0,15},{1,2},{2,1},{3,4},{4,3},{5,6},{6,5},{7,8},{8,7},{9,10},{10,... | collective-permute-start | bytes 602120 | tf_op jit(solution)/shard_map/ppermute | solution.py:50
  171.5 26.8 %collective-permute-start.46 = (f32[5,8,1536]{2,1,0:T(8,128)S(1)}, f32[5,8,1536]{2,1,0:T(8,128)S(1)}, u32[]{:S(2)}, u32[]{:S(2)}) collective-permute-start(f32[5,8,1536]{2,1,0:T(8,128)S(1)} %copy-done.39), channel_id=1, source_target_pairs={{0,16},{16,0},{32,48},{48,32},{64,80},{80,64},{96,112},{112,96},{1... | collective-permute-start | bytes 737288 | tf_op jit(solution)/shard_map/ppermute | solution.py:50
  182.8 11.1 %collective-permute-start.42 = (f32[200,128]{1,0:T(8,128)S(1)}, f32[200,128]{1,0:T(8,128)S(1)}, u32[]{:S(2)}, u32[]{:S(2)}) collective-permute-start(f32[200,128]{1,0:T(8,128)S(1)} %get-tuple-element.150), channel_id=1, source_target_pairs={{0,1},{1,0},{2,3},{3,2},{4,5},{5,4},{6,7},{7,6},{8,9},{9,8},{10,11... | collective-permute-start | bytes 307208 | tf_op jit(solution)/shard_map/ppermute | solution.py:50
  182.9 11.0 %collective-permute-start.43 = (f32[200,128]{1,0:T(8,128)S(1)}, f32[200,128]{1,0:T(8,128)S(1)}, u32[]{:S(2)}, u32[]{:S(2)}) collective-permute-start(f32[200,128]{1,0:T(8,128)S(1)} %get-tuple-element.151), channel_id=1, source_target_pairs={{0,15},{1,2},{2,1},{3,4},{4,3},{5,6},{6,5},{7,8},{8,7},{9,10},{10,... | collective-permute-start | bytes 307208 | tf_op jit(solution)/shard_map/ppermute | solution.py:50
  196.7 18.1 %collective-permute-start.48 = (f32[200,128]{1,0:T(8,128)S(1)}, f32[200,128]{1,0:T(8,128)S(1)}, u32[]{:S(2)}, u32[]{:S(2)}) collective-permute-start(f32[200,128]{1,0:T(8,128)S(1)} %get-tuple-element.161), channel_id=1, source_target_pairs={{0,1},{1,0},{2,3},{3,2},{4,5},{5,4},{6,7},{7,6},{8,9},{9,8},{10,11... | collective-permute-start | bytes 307208 | tf_op jit(solution)/shard_map/ppermute | solution.py:50
  196.7 18.1 %collective-permute-start.49 = (f32[200,128]{1,0:T(8,128)S(1)}, f32[200,128]{1,0:T(8,128)S(1)}, u32[]{:S(2)}, u32[]{:S(2)}) collective-permute-start(f32[200,128]{1,0:T(8,128)S(1)} %get-tuple-element.162), channel_id=1, source_target_pairs={{0,15},{1,2},{2,1},{3,4},{4,3},{5,6},{6,5},{7,8},{8,7},{9,10},{10,... | collective-permute-start | bytes 307208 | tf_op jit(solution)/shard_map/ppermute | solution.py:50
  198.3 16.5 %collective-permute-start.50 = (f32[1,8,1536]{2,1,0:T(8,128)S(1)}, f32[1,8,1536]{2,1,0:T(8,128)S(1)}, u32[]{:S(2)}, u32[]{:S(2)}) collective-permute-start(f32[1,8,1536]{2,1,0:T(8,128)S(1)} %get-tuple-element.163), channel_id=1, source_target_pairs={{0,16},{16,0},{32,48},{48,32},{64,80},{80,64},{96,112},{112,96},{1... | collective-permute-start | bytes 147464 | tf_op jit(solution)/shard_map/ppermute | solution.py:50
  198.3 16.5 %collective-permute-start.51 = (f32[1,8,1536]{2,1,0:T(8,128)S(1)}, f32[1,8,1536]{2,1,0:T(8,128)S(1)}, u32[]{:S(2)}, u32[]{:S(2)}) collective-permute-start(f32[1,8,1536]{2,1,0:T(8,128)S(1)} %get-tuple-element.164), channel_id=1, source_target_pairs={{0,112},{16,32},{32,16},{48,64},{64,48},{80,96},{96,80},{112,0},{1... | collective-permute-start | bytes 147464 | tf_op jit(solution)/shard_map/ppermute | solution.py:50
  (85 other events, 580.2 us)

commit v3 on v0

v3 whole, which is shorter than its diff:
```python
import functools

import jax
import jax.numpy as jnp
from jax import lax
from jax.experimental import pallas as pl
from jax.experimental.pallas import tpu as pltpu
from jax.sharding import PartitionSpec as P

F32 = jnp.float32
STEPS = 5
CHEB = 6
CZ, CX, NY = 16, 8, 1536
TILES = NY // 128
ZR = TILES * CX
XR = TILES * CZ
ROWS = CZ * ZR
OWN = 8 + ZR
WIN = 64
SPAN = 6
PRIOR = 288
SHIFT = 0.5
EXACT = lax.Precision.HIGHEST

VM = pl.BlockSpec(memory_space=pltpu.VMEM)
SM = pl.BlockSpec(memory_space=pltpu.SMEM)
ANY = pl.BlockSpec(memory_space=pl.ANY)


def shape(*dims):
    return jax.ShapeDtypeStruct(dims, F32)


def call(body, outs, ins, scratch=(), limit=6, flops=4 * 10**6, traffic=5 * 10**6):
    return pl.pallas_call(
        body,
        out_shape=outs,
        in_specs=ins,
        out_specs=jax.tree.map(lambda _: VM, outs),
        scratch_shapes=list(scratch),
        compiler_params=pltpu.CompilerParams(vmem_limit_bytes=limit * 2**20),
        cost_estimate=pl.CostEstimate(flops=flops, bytes_accessed=traffic, transcendentals=0),
    )


def pairs_a(n):
    return [(i, i ^ 1) for i in range(n)]


def pairs_b(n):
    return [(i, (((i + 1) ^ 1) - 1) % n) for i in range(n)]


def swap(send, axis):
    n = lax.axis_size(axis)
    return lax.ppermute(send[0], axis, pairs_a(n)), lax.ppermute(send[1], axis, pairs_b(n))


def to_sides(info, k, first, second):
    odd = info[k] == 1
    below = jnp.where(info[2 + 2 * k] == 1, jnp.where(odd, first, second), 0.0)
    above = jnp.where(info[3 + 2 * k] == 1, jnp.where(odd, second, first), 0.0)
    return below, above


def from_sides(info, k, below, above):
    odd = info[k] == 1
    return jnp.where(odd, below, above), jnp.where(odd, above, below)


def put_x(info, refs, to, field, base):
    for t in range(TILES):
        low = field[pl.ds(base + t * CX, CZ, stride=ZR), :]
        high = field[pl.ds(base + t * CX + CX - 1, CZ, stride=ZR), :]
        first, second = from_sides(info, 0, low, high)
        refs[0][to + t * CZ : to + (t + 1) * CZ, :] = first
        refs[1][to + t * CZ : to + (t + 1) * CZ, :] = second


def put_z(info, refs, to, field, base):
    first, second = from_sides(info, 1, field[base : base + ZR, :], field[base + ROWS - ZR : base + ROWS, :])
    refs[0][to : to + ZR, :] = first
    refs[1][to : to + ZR, :] = second


def load_sides(info, rx, base, side):
    side[...] = jnp.zeros_like(side)
    for t in range(TILES):
        at = base + t * CZ
        low, high = to_sides(info, 0, rx[0][at : at + CZ, :], rx[1][at : at + CZ, :])
        side[pl.ds(t * CX, CZ, stride=ZR), :] = low
        side[pl.ds(t * CX + CX - 1, CZ, stride=ZR), :] = high


def load_ext(info, field, base, rz, at, ext):
    ext[OWN : OWN + ROWS, :] = field[base : base + ROWS, :]
    low, high = to_sides(info, 1, rz[0][at : at + ZR, :], rz[1][at : at + ZR, :])
    ext[OWN - ZR : OWN, :] = low
    ext[OWN + ROWS : OWN + ROWS + ZR, :] = high


def pass_peak(mine, rx, at, sends, to, out):
    best = mine[...]
    if at is not None:
        best = jnp.maximum(best, jnp.maximum(rx[0][at : at + 8, :], rx[1][at : at + 8, :]))
    out[...] = best
    if sends is not None:
        for send in sends:
            send[to : to + 8, :] = best


EXT = pltpu.VMEM((OWN + ROWS + ZR + 8, 128), F32)
SIDE = pltpu.VMEM((ROWS, 128), F32)


def iota(axis):
    return lax.broadcasted_iota(jnp.int32, (CX, 128), axis)


def lanes_up(tiles, lane):
    moved = [pltpu.roll(v, 127, 1) for v in tiles]
    return [jnp.where(lane == 127, moved[(t + 1) % TILES], moved[t]) for t in range(TILES)]


def lanes_down(tiles, lane):
    moved = [pltpu.roll(v, 1, 1) for v in tiles]
    return [jnp.where(lane == 0, moved[t - 1], moved[t]) for t in range(TILES)]


def rows_of(z, t):
    return pl.multiple_of(z * ZR + t * CX, CX)


def tile(ref, row, offset=0):
    return ref[pl.ds(row + offset, CX), :]


def each_layer(body):
    def step(z, carry):
        body(z)
        return carry

    lax.fori_loop(0, CZ, step, 0)


GROUP = 4


def scatter(info, code, misfit, cond, prior, out, xa, xb, za, zb):
    out[...] = jnp.zeros_like(out)
    place = iota(0) * 128 + iota(1)

    def step(i, carry):
        codes = [code[i * GROUP + k] for k in range(GROUP)]
        at = [lax.shift_right_logical(c, 10) * CX for c in codes]
        adds = [jnp.where(place == (c & 1023), misfit[i * GROUP + k], 0.0) for k, c in enumerate(codes)]
        sums = [tile(out, pl.multiple_of(a, CX)) for a in at]
        for k in range(GROUP):
            total = sums[k] + adds[k]
            for j in range(k):
                total = total + jnp.where(at[j] == at[k], adds[j], 0.0)
            out[pl.ds(pl.multiple_of(at[k], CX), CX), :] = total
        return carry

    lax.fori_loop(0, code.shape[0] // GROUP, step, 0, unroll=8)
    base = (STEPS - 1) * ROWS
    put_x(info, (xa, xb), 0, out, base)
    put_x(info, (xa, xb), XR, cond, 0)
    xa[2 * XR :, :] = prior[...]
    xb[2 * XR :, :] = prior[...]
    put_z(info, (za, zb), 0, out, base)
    put_z(info, (za, zb), ZR, cond, 0)


def faces(info, cond, rxa, rxb, rza, rzb, fz, fy, fxh, fxl, fxb, inv, ext, side):
    load_ext(info, cond, 0, (rza, rzb), ZR, ext)
    load_sides(info, (rxa, rxb), XR, side)
    sub, lane = iota(0), iota(1)

    def layer(z):
        rows = [rows_of(z, t) for t in range(TILES)]
        cs = [tile(ext, r, OWN) for r in rows]
        ups = lanes_up(cs, lane)
        ups[-1] = jnp.where(lane == 127, 0.0, ups[-1])
        y_hi = [0.5 * (c + u) for c, u in zip(cs, ups)]
        y_lo = lanes_down(y_hi, lane)
        y_lo[0] = jnp.where(lane == 0, 0.5 * cs[0], y_lo[0])
        for t, r in enumerate(rows):
            c = cs[t]
            here = pl.ds(r, CX)
            beside = tile(side, r)
            z_lo = 0.5 * (c + tile(ext, r, OWN - ZR))
            z_hi = 0.5 * (c + tile(ext, r, OWN + ZR))
            x_hi = 0.5 * (c + jnp.where(sub == CX - 1, beside, tile(ext, r, OWN + 1)))
            x_lo = 0.5 * (c + jnp.where(sub == 0, beside, tile(ext, r, OWN - 1)))
            fz[here, :] = z_lo
            fz[pl.ds(r + ZR, CX), :] = z_hi
            fy[here, :] = jnp.where(lane == 127, 0.0, y_hi[t]) if t == TILES - 1 else y_hi[t]
            fxh[here, :] = jnp.where(sub == CX - 1, 0.0, x_hi)
            fxl[here, :] = jnp.where(sub == 0, 0.0, x_lo)
            fxb[here, :] = jnp.where(sub == CX - 1, x_hi, jnp.where(sub == 0, x_lo, 0.0))
            inv[here, :] = 1.0 / (1.0 + (((((z_hi + z_lo) + x_hi) + x_lo) + y_hi[t]) + y_lo[t]))

    each_layer(layer)


def sweep(right, base, fz, fy, fxh, fxl, fxb, inv, ext, side, lane, z):
    rows = [rows_of(z, t) for t in range(TILES)]
    vs = [tile(ext, r, OWN) for r in rows]
    ys = [tile(fy, r) for r in rows]
    ups = lanes_up(vs, lane)
    downs = lanes_down([y * v for y, v in zip(ys, vs)], lane)
    new = []
    for t, r in enumerate(rows):
        spread = tile(fz, r, ZR) * tile(ext, r, OWN + ZR) + tile(fz, r) * tile(ext, r, OWN - ZR)
        spread = spread + (tile(fxh, r) * tile(ext, r, OWN + 1) + tile(fxl, r) * tile(ext, r, OWN - 1))
        spread = spread + tile(fxb, r) * tile(side, r)
        spread = spread + (ys[t] * ups[t] + downs[t])
        new.append((tile(right, r, base) + spread) * tile(inv, r))
    return rows, new


def first_sweep(n, info, peak, forcing, fwd, low, high, *refs):
    first = n == STEPS - 1
    fz, fy, fxh, fxl, fxb, inv, rxa, rxb, rza, rzb, out, known, xa, xb, za, zb, ext, side = refs
    base = (STEPS - 1) * ROWS if first else 0
    pass_peak(peak, (rxa, rxb), None if first else 2 * XR, (xa, xb), 2 * XR, known)
    load_ext(info, forcing, base, (rza, rzb), 0 if first else ZR, ext)
    load_sides(info, (rxa, rxb), 0 if first else XR, side)
    lane = iota(1)

    def layer(z):
        rows, new = sweep(forcing, base, fz, fy, fxh, fxl, fxb, inv, ext, side, lane, z)
        for r, v in zip(rows, new):
            out[pl.ds(r, CX), :] = v

    each_layer(layer)
    put_x(info, (xa, xb), 0, out, 0)
    put_z(info, (za, zb), 0, out, 0)
    put_x(info, (xa, xb), XR, fwd, n * ROWS)
    put_z(info, (za, zb), ZR, fwd, n * ROWS)
    if first:
        one, two = from_sides(info, 1, low[...], high[...])
        za[2 * ZR :, :] = one
        zb[2 * ZR :, :] = two


def second_sweep(n, info, peak, v, forcing, source, earlier, *refs):
    fz, fy, fxh, fxl, fxb, inv, rxa, rxb, rza, rzb, out, after, known, xa, xb, za, zb, ext, side = refs
    base = (STEPS - 1) * ROWS if n == STEPS - 1 else 0
    pass_peak(peak, (rxa, rxb), 2 * XR, (xa, xb), 2 * XR if n else XR, known)
    load_ext(info, v, 0, (rza, rzb), 0, ext)
    load_sides(info, (rxa, rxb), 0, side)
    lane = iota(1)

    def layer(z):
        rows, new = sweep(forcing, base, fz, fy, fxh, fxl, fxb, inv, ext, side, lane, z)
        for r, v in zip(rows, new):
            out[pl.ds(r, CX), :] = v
            if n:
                after[pl.ds(r, CX), :] = v + tile(source, r, (n - 1) * ROWS)

    each_layer(layer)
    put_x(info, (xa, xb), 0, out, 0)
    put_z(info, (za, zb), 0, out, 0)
    if n:
        put_x(info, (xa, xb), XR, after, 0)
        put_z(info, (za, zb), ZR, after, 0)


def gradient(n, info, a_ref, f_ref, acc, *refs):
    rxa, rxb, rza, rzb, fxa, fxb, fza, fzb, out, a_ext, f_ext, a_side, f_side = refs
    load_ext(info, a_ref, 0, (rza, rzb), 0, a_ext)
    load_sides(info, (rxa, rxb), 0, a_side)
    load_ext(info, f_ref, n * ROWS, (fza, fzb), ZR, f_ext)
    load_sides(info, (fxa, fxb), XR, f_side)
    sub, lane = iota(0), iota(1)

    def layer(z):
        rows = [rows_of(z, t) for t in range(TILES)]
        a_s = [tile(a_ext, r, OWN) for r in rows]
        f_s = [tile(f_ext, r, OWN) for r in rows]
        a_up, f_up = lanes_up(a_s, lane), lanes_up(f_s, lane)
        a_up[-1] = jnp.where(lane == 127, 0.0, a_up[-1])
        f_up[-1] = jnp.where(lane == 127, 0.0, f_up[-1])
        y_hi = [(a - au) * (f - fu) for a, au, f, fu in zip(a_s, a_up, f_s, f_up)]
        y_lo = lanes_down(y_hi, lane)
        y_lo[0] = jnp.where(lane == 0, a_s[0] * f_s[0], y_lo[0])
        for t, r in enumerate(rows):
            a, f = a_s[t], f_s[t]
            total = y_hi[t] + y_lo[t]
            for step in (ZR, -ZR):
                total = total + (a - tile(a_ext, r, OWN + step)) * (f - tile(f_ext, r, OWN + step))
            for step, edge in ((1, CX - 1), (-1, 0)):
                a_by = jnp.where(sub == edge, tile(a_side, r), tile(a_ext, r, OWN + step))
                f_by = jnp.where(sub == edge, tile(f_side, r), tile(f_ext, r, OWN + step))
                total = total + (a - a_by) * (f - f_by)
            out[pl.ds(r, CX), :] = total if n == STEPS - 1 else tile(acc, r) + total

    each_layer(layer)


def coarsen(acc, cond, peak, rxa, rxb, out, known, fine, rows, tall):
    pass_peak(peak, (rxa, rxb), XR, None, None, known)
    fine[...] = -0.5 * cond[...] * acc[...]
    for t in range(TILES):
        for p in range(2):
            total = None
            for x in range(4):
                part = fine[pl.ds(t * CX + 4 * p + x, CZ, stride=ZR), :]
                total = part if total is None else total + part
            rows[p * CZ : (p + 1) * CZ, t * 128 : (t + 1) * 128] = total
    group = lax.broadcasted_iota(jnp.int32, (128, 512), 1) // 4
    pick = jnp.where(group == lax.broadcasted_iota(jnp.int32, (128, 512), 0), 1.0, 0.0)
    tall[...] = jnp.zeros_like(tall)
    for k in range(3):
        tall[8 + 128 * k : 8 + 128 * (k + 1), :] = lax.dot_general(
            pick,
            rows[:, 512 * k : 512 * (k + 1)],
            (((1,), (1,)), ((), ())),
            precision=EXACT,
            preferred_element_type=F32,
        )
    for d in range(out.shape[0]):
        out[d, 0:WIN] = tall[48 * d : 48 * d + WIN, :]
        out[d, WIN : WIN + 8] = known[:, : 2 * CZ]


def assemble(pieces, window, coarse, upper):
    best = pieces[0, WIN : WIN + 8]
    for d in range(1, pieces.shape[0]):
        best = jnp.maximum(best, pieces[d, WIN : WIN + 8])
    upper[...] = best
    k = lax.broadcasted_iota(jnp.int32, (2 * CZ, 128), 0)
    z = lax.broadcasted_iota(jnp.int32, (2 * CZ, 128), 1)
    for p in range(2):
        total = jnp.zeros((WIN, 128), F32)
        for d in range(pieces.shape[0]):
            own = (z >= CZ * d) & (z < CZ * (d + 1)) & (k - CZ * p == z - CZ * d)
            total = total + jnp.dot(
                pieces[d, 0:WIN], jnp.where(own, 1.0, 0.0), precision=EXACT, preferred_element_type=F32
            )
        window[p * WIN : (p + 1) * WIN, :] = total
        coarse[p] = total[8:56]


def prior_setup(place, w, fx, fy, fz, diag, peak):
    first_column, first_row = place[0], place[1]
    row = lax.broadcasted_iota(jnp.int32, (WIN, 128), 0)
    lane = lax.broadcasted_iota(jnp.int32, (WIN, 128), 1)
    y_in = (row + first_row >= 0) & (row + first_row < 384)
    y_link = y_in & (row + first_row + 1 >= 0) & (row + first_row + 1 < 384) & (row < WIN - 1)

    def x_in(j):
        return (first_column + j >= 0) & (first_column + j < 32)

    def wx(j):
        if j < 0 or j >= SPAN:
            return jnp.zeros((WIN, 128), F32)
        return jnp.where(x_in(j) & y_in, w[0, j], 0.0)

    best = None
    for j in range(SPAN):
        inside = x_in(j) & y_in
        here = wx(j)
        x_hi = 0.5 * (here + wx(j + 1))
        x_lo = 0.5 * (here + wx(j - 1))
        v = jnp.where(inside, w[1, j], 0.0)
        y_hi = 0.5 * (v + jnp.where(row == WIN - 1, 0.0, pltpu.roll(v, WIN - 1, 0)))
        y_lo = jnp.where(row == 0, 0.5 * v, pltpu.roll(y_hi, 1, 0))
        v = jnp.where(inside, w[2, j], 0.0)
        z_hi = 0.5 * (v + jnp.where(lane == 127, 0.0, pltpu.roll(v, 127, 1)))
        z_lo = jnp.where(lane == 0, 0.5 * v, pltpu.roll(z_hi, 1, 1))
        total = ((((x_hi + x_lo) + y_hi) + y_lo) + z_hi) + z_lo
        diag[j] = SHIFT + total
        fx[j] = jnp.where(inside & x_in(j + 1), x_hi, 0.0) if j + 1 < SPAN else jnp.zeros_like(x_hi)
        fy[j] = jnp.where(x_in(j) & y_link, y_hi, 0.0)
        fz[j] = jnp.where(inside & (lane < 127), z_hi, 0.0)
        if j in (2, 3):
            bound = jnp.max((SHIFT + 2.0 * total)[8:56].reshape(6, 8, 128), axis=0)
            best = bound if best is None else jnp.maximum(best, bound)
    peak[...] = jnp.full((8, 128), jnp.max(best))


def coefficients(upper):
    top = upper[0:1, 0:1]
    centre = 0.5 * (top + SHIFT)
    half = 0.5 * (top - SHIFT)
    sigma = centre / half
    rho = 1.0 / sigma
    scales = []
    for _ in range(CHEB - 1):
        rho_new = 1.0 / (2.0 * sigma - rho)
        scales.append((rho_new * rho, 2.0 * rho_new / half))
        rho = rho_new
    return centre, scales


def cheb_column(j, scale, r, d, prior):
    fx, fy, fz, diag = prior
    v = d[j]
    y_face, z_face = fy[j], fz[j]
    pull = fx[j] * d[j + 1] + fx[j - 1] * d[j - 1]
    pull = pull + y_face * pltpu.roll(v, WIN - 1, 0) + pltpu.roll(y_face * v, 1, 0)
    pull = pull + z_face * pltpu.roll(v, 127, 1) + pltpu.roll(z_face * v, 1, 1)
    left = r[j] - (diag[j] * v - pull)
    return left, scale[0] * v + scale[1] * left


def block(ref, k):
    return ref[k * WIN : (k + 1) * WIN, :]


def cheb_send(info, d, r, sa, sb):
    for k, (low, high) in enumerate(((d[2], d[2]), (d[3], d[3]), (r[2], r[3]))):
        one, two = from_sides(info, 0, low, high)
        sa[k * WIN : (k + 1) * WIN, :] = one
        sb[k * WIN : (k + 1) * WIN, :] = two


def cheb_two(first, r, d, scales, prior):
    r, d = dict(r), dict(d)
    sums = []
    for it in range(2):
        fresh = {}
        for j in range(1 + it, SPAN - 1 - it):
            r[j], fresh[j] = cheb_column(j, scales[first + it], r, d, prior)
        d = fresh
        sums.append((d[2], d[3]))
    return r, d, sums


def cheb_one(info, upper, g, ra, rb, fx, fy, fz, diag, out, r_out, d_out, sa, sb):
    centre, scales = coefficients(upper)
    r = {2: block(g, 0), 3: block(g, 1)}
    for k in range(2):
        r[k], r[4 + k] = to_sides(info, 0, block(ra, k), block(rb, k))
    d = {j: v / centre for j, v in r.items()}
    start = (d[2], d[3])
    r, d, sums = cheb_two(0, r, d, scales, (fx, fy, fz, diag))
    for p in range(2):
        out[p] = ((start[p] + sums[0][p]) + sums[1][p])[8:56]
        r_out[p], d_out[p] = r[2 + p], d[2 + p]
    cheb_send(info, d, r, sa, sb)


def cheb_mid(info, upper, x, r_in, d_in, ra, rb, fx, fy, fz, diag, out, r_out, d_out, sa, sb):
    _, scales = coefficients(upper)
    r, d = {2: r_in[0], 3: r_in[1]}, {2: d_in[0], 3: d_in[1]}
    for k in range(2):
        d[k], d[4 + k] = to_sides(info, 0, block(ra, k), block(rb, k))
    r[1], r[4] = to_sides(info, 0, block(ra, 2), block(rb, 2))
    r, d, sums = cheb_two(2, r, d, scales, (fx, fy, fz, diag))
    for p in range(2):
        out[p] = (x[p] + sums[0][p][8:56]) + sums[1][p][8:56]
        r_out[p], d_out[p] = r[2 + p], d[2 + p]
    one, two = from_sides(info, 0, d[2], d[3])
    sa[...] = one
    sb[...] = two


def cheb_last(info, upper, x, r_in, d_in, ra, rb, fx, fy, fz, diag, out):
    _, scales = coefficients(upper)
    r, d = {2: r_in[0], 3: r_in[1]}, {2: d_in[0], 3: d_in[1]}
    d[1], d[4] = to_sides(info, 0, ra[...], rb[...])
    for p in range(2):
        _, new = cheb_column(2 + p, scales[4], r, d, (fx, fy, fz, diag))
        out[p] = x[p] + new[8:56]


def as_rows(field):
    lead = field.shape[:-2]
    return jnp.swapaxes(field.reshape(*lead, CX, TILES, 128), -3, -2).reshape(-1, 128)


def on_device(
    conductivity, forward_states, sensor_cell, sensor_window, sensor_misfit, prior_conductance
):
    z_at, x_at = lax.axis_index("depth"), lax.axis_index("strip")
    z_n, x_n = lax.axis_size("depth"), lax.axis_size("strip")
    info = jnp.stack(
        [
            x_at % 2,
            z_at % 2,
            (x_at > 0).astype(jnp.int32),
            (x_at < x_n - 1).astype(jnp.int32),
            (z_at > 0).astype(jnp.int32),
            (z_at < z_n - 1).astype(jnp.int32),
        ]
    ).astype(jnp.int32)
    place = jnp.stack([2 * x_at - 2, 48 * z_at - 8]).astype(jnp.int32)
    x_odd, z_odd = x_at % 2 == 1, z_at % 2 == 1
    cond = as_rows(conductivity)
    fwd = as_rows(forward_states)
    field, small = shape(ROWS, 128), shape(8, 128)

    layer = sensor_window * CZ + sensor_cell // (CX * NY)
    lateral = sensor_cell % NY
    code = (layer * TILES + lateral // 128) * 1024 + (sensor_cell // NY) % CX * 128 + lateral % 128
    xs, zs = shape(2 * XR + PRIOR, 128), shape(2 * ZR, 128)
    sources, xa, xb, za, zb = call(
        scatter, (shape(STEPS * ROWS, 128), xs, xs, zs, zs), [SM, SM, SM, VM, VM], flops=4 * 10**7
    )(info, code, sensor_misfit, cond, prior_conductance.reshape(PRIOR, 128))
    rx, rz = swap((xa, xb), "strip"), swap((za, zb), "depth")
    table = call(
        faces, (shape(ROWS + ZR, 128),) + (field,) * 5, [SM] + [VM] * 5, [EXT, SIDE]
    )(info, cond, *rx, *rz)
    above = jnp.where(x_odd, rx[1][2 * XR :], rx[0][2 * XR :]).reshape(3, 2, 48, 128)
    below = jnp.where(x_odd, rx[0][2 * XR :], rx[1][2 * XR :]).reshape(3, 2, 48, 128)
    weights = jnp.concatenate([below, prior_conductance, above], axis=1)
    low, high = weights[:, :, :8].reshape(144, 128), weights[:, :, 40:].reshape(144, 128)

    forcing = sources
    known = jnp.zeros((8, 128), F32)
    acc = known
    waiting = None
    for n in reversed(range(STEPS)):
        first = n == STEPS - 1
        xs, zs = shape(2 * XR + 8, 128), shape(2 * ZR + (144 if first else 0), 128)
        v, known, xa, xb, za, zb = call(
            functools.partial(first_sweep, n),
            (field, small, xs, xs, zs, zs),
            [SM] + [VM] * 3 + [VM if first else ANY] * 2 + [VM] * 10,
            [EXT, SIDE],
        )(info, known, forcing, fwd, low, high, *table, *rx, *rz)
        rx, rz = swap((xa, xb), "strip"), swap((za, zb), "depth")
        if first:
            tails = rz[0][2 * ZR :], rz[1][2 * ZR :]
            under = jnp.where(z_odd, tails[0], tails[1]).reshape(3, SPAN, 8, 128)
            over = jnp.where(z_odd, tails[1], tails[0]).reshape(3, SPAN, 8, 128)
            span = shape(SPAN, WIN, 128)
            *prior, peak = call(prior_setup, (span, span, span, span, small), [SM, VM])(
                place, jnp.concatenate([under, weights, over], axis=2)
            )
        if waiting is not None:
            acc = waiting()
        forward_x, forward_z = rx, rz
        fields = 2 if n else 1
        xs, zs = shape(fields * XR + 8, 128), shape(fields * ZR, 128)
        adjoint, after, known, xa, xb, za, zb = call(
            functools.partial(second_sweep, n),
            (field, field if n else small, small, xs, xs, zs, zs),
            [SM] + [VM] * 3 + [VM if n else ANY, ANY] + [VM] * 10,
            [EXT, SIDE],
        )(info, known, v, forcing, sources, acc, *table, *rx, *rz)
        rx, rz = swap((xa, xb), "strip"), swap((za, zb), "depth")

        def waiting(n=n, adjoint=adjoint, acc=acc, halos=(*rx, *rz, *forward_x, *forward_z)):
            return call(
                functools.partial(gradient, n),
                field,
                [SM] + [VM] * 2 + [ANY if n == STEPS - 1 else VM] + [VM] * 8,
                [EXT, EXT, SIDE, SIDE],
            )(info, adjoint, fwd, acc, *halos)

        if first:
            known = peak
        forcing = after
    acc = waiting()

    pieces, _ = call(
        coarsen,
        (shape(z_n, WIN + 8, 2 * CZ), small),
        [VM] * 5,
        [SIDE, pltpu.VMEM((2 * CZ, NY), F32), pltpu.VMEM((400, 2 * CZ), F32)],
    )(acc, cond, known, *rx)
    pieces = lax.all_to_all(pieces, "depth", 0, 0)
    window, coarse_grad, upper = call(
        assemble, (shape(2 * WIN, 128), shape(2, 48, 128), shape(8, 2 * CZ)), [VM]
    )(pieces)

    own, both = shape(2, 48, 128), shape(2, WIN, 128)
    sides = swap((window, window), "strip")
    x, r, d, sa, sb = call(
        cheb_one, (own, both, both, shape(3 * WIN, 128), shape(3 * WIN, 128)), [SM] + [VM] * 8
    )(info, upper, window, *sides, *prior)
    sides = swap((sa, sb), "strip")
    x, r, d, sa, sb = call(
        cheb_mid, (own, both, both, shape(WIN, 128), shape(WIN, 128)), [SM] + [VM] * 10
    )(info, upper, x, r, d, *sides, *prior)
    sides = swap((sa, sb), "strip")
    step = call(cheb_last, own, [SM] + [VM] * 10)(info, upper, x, r, d, *sides, *prior)
    return coarse_grad, step


def solution(mesh):
    placed = (
        P("depth", "strip", None),
        P(None, "depth", "strip", None),
        P(("depth", "strip")),
        P(("depth", "strip")),
        P(("depth", "strip")),
        P(None, "strip", "depth", None),
    )
    return jax.shard_map(
        on_device,
        mesh=mesh,
        in_specs=placed,
        out_specs=(P("strip", "depth", None), P("strip", "depth", None)),
        check_vma=False,
    )
```

time: 615 us -> 253 us (0.41)
  the two profiles are of different devices: /device:TPU:10 before, /device:TPU:0 now
where the time goes in v3:
time: 253 us; the launch traced here: 252 us
  Pallas kernels  74.3 us (29%)
  waiting for transfers between devices  68.2 us (27%)
  starting transfers between devices  67.9 us (27%)
  local copies, waits for them, and re-layouts  29 us (11%)
  blocking collectives  9.97 us (4%)
    ppermute x25, starting transfers between devices, swap(): lax.ppermute(send[1], axis, pairs_b(n))  62.8 us
    ppermute x25, waiting for transfers between devices, swap(): lax.ppermute(send[1], axis, pairs_b(n))  45.5 us
    unnamed x88, local copies, waits for them, and re-layouts  28.6 us
    ppermute x25, waiting for transfers between devices, swap(): lax.ppermute(send[0], axis, pairs_a(n))  22.8 us
    pallas_call x5, Pallas kernels, waiting(): call(functools.partial(gradient, n), field, [SM] + [VM] * 2 + [ANY if n =...  19.8 us
    pallas_call x1, Pallas kernels, on_device(): call(scatter, (shape(STEPS * ROWS, 128), xs, xs, zs, zs), [SM, SM, SM, VM...  15.2 us
    pallas_call x5, Pallas kernels, on_device(): call(functools.partial(second_sweep, n), (field, field if n else small, s...  15 us
    pallas_call x5, Pallas kernels, on_device(): call(functools.partial(first_sweep, n), (field, small, xs, xs, zs, zs), [...  14.2 us
  transfers between devices with their start and end apart: 50, of which 26 were waited for; matrix products, arithmetic and copies ran while one was open for 0% of the time, Pallas kernels for 7%

profile of v3, /device:TPU:0, one launch (start us, length us, event | category | flops | bytes accessed | tf_op | source)
XLA Modules:
  0.0 252.3 jit_solution(4481184358304147429)
XLA Ops:
  4.3 15.2 %shard_map.77 = (f32[7680,128]{1,0:T(8,128)S(1)}, f32[672,128]{1,0:T(8,128)S(1)}, f32[672,128]{1,0:T(8,128)S(1)}, f32[192,128]{1,0:T(8,128)S(1)}, f32[192,128]{1,0:T(8,128)S(1)}) custom-call(s32[6]{0:T(128)S(1)} %stack.52.info, s32[4096]{0:T(1024)S(1)} %fusion.5.code, f32[4096]{0:T(1024)S(1)} %copy-done.39, f32[1536,128]{1,0:T(8,128)S(1)} %bitcast.35, ...), custom_call_target="tpu_custom_call" | custom-call | flops 40000000 | bytes 5000000 | tf_op jit(solution)/shard_map/pallas_call | solution.py:501
  21.4 5.6 %collective-permute-start.1 = (f32[672,128]{1,0:T(8,128)S(1)}, f32[672,128]{1,0:T(8,128)S(1)}, u32[]{:S(2)}, u32[]{:S(2)}) collective-permute-start(f32[672,128]{1,0:T(8,128)S(1)} %get-tuple-element.97), channel_id=1, source_target_pairs={{0,15},{1,2},{2,1},{3,4},{4,3},{5,6},{6,5},{7,8},{8,7},{9,10},{10,... | collective-permute-start | bytes 1032200 | tf_op jit(solution)/shard_map/ppermute | solution.py:56
  61.2 4.4 %collective-permute-start.7 = (f32[392,128]{1,0:T(8,128)}, f32[392,128]{1,0:T(8,128)}, u32[]{:S(2)}, u32[]{:S(2)}) collective-permute-start(f32[392,128]{1,0:T(8,128)} %get-tuple-element.112), channel_id=1, source_target_pairs={{0,15},{1,2},{2,1},{3,4},{4,3},{5,6},{6,5},{7,8},{8,7},{9,10},{10,... | collective-permute-start | bytes 602120 | tf_op jit(solution)/shard_map/ppermute | solution.py:56
  80.2 4.0 %shard_map.81 = (f32[1536,128]{1,0:T(8,128)S(1)}, f32[1536,128]{1,0:T(8,128)S(1)}, f32[8,128]{1,0:T(8,128)}, f32[392,128]{1,0:T(8,128)S(1)}, f32[392,128]{1,0:T(...) custom-call(s32[6]{0:T(128)S(1)} %stack.52.info, f32[8,128]{1,0:T(8,128)S(1)} %get-tuple-element.109.peak, ...), custom_call_target="tpu_custom_call" | custom-call | flops 4000000 | bytes 5000000 | tf_op jit(solution)/shard_map/pallas_call | solution.py:540
  84.2 4.2 %collective-permute-start.9 = (f32[392,128]{1,0:T(8,128)S(1)}, f32[392,128]{1,0:T(8,128)S(1)}, u32[]{:S(2)}, u32[]{:S(2)}) collective-permute-start(f32[392,128]{1,0:T(8,128)S(1)} %get-tuple-element.115), channel_id=1, source_target_pairs={{0,15},{1,2},{2,1},{3,4},{4,3},{5,6},{6,5},{7,8},{8,7},{9,10},{10,... | collective-permute-start | bytes 602120 | tf_op jit(solution)/shard_map/ppermute | solution.py:56
  99.0 4.5 %collective-permute-start.13 = (f32[392,128]{1,0:T(8,128)S(1)}, f32[392,128]{1,0:T(8,128)S(1)}, u32[]{:S(2)}, u32[]{:S(2)}) collective-permute-start(f32[392,128]{1,0:T(8,128)S(1)} %get-tuple-element.122), channel_id=1, source_target_pairs={{0,15},{1,2},{2,1},{3,4},{4,3},{5,6},{6,5},{7,8},{8,7},{9,10},{10,... | collective-permute-start | bytes 602120 | tf_op jit(solution)/shard_map/ppermute | solution.py:56
  104.1 4.4 %shard_map.83.earlier.acc = f32[1536,128]{1,0:T(8,128)S(1)} custom-call(s32[6]{0:T(128)S(1)} %stack.52.info, f32[1536,128]{1,0:T(8,128)S(1)} %get-tuple-element.120.a_ref, f32[7680,128]{1,0:T(8,128)S(1)} %bitcast.27, f32[8,128]{1,0:T(8,128)S(1)} %broadcast_in_dim.3.peak.earlier.acc, f32[392,128]{1,0:T(8,128)S(1)} %collective-permute-done.8.refs_6_.refs_0_, ...), custom_call_target="tpu_custom_call" | custom-call | flops 4000000 | bytes 5000000 | tf_op jit(solution)/shard_map/pallas_call | solution.py:549
  113.1 4.6 %collective-permute-start.17 = (f32[392,128]{1,0:T(8,128)S(1)}, f32[392,128]{1,0:T(8,128)S(1)}, u32[]{:S(2)}, u32[]{:S(2)}) collective-permute-start(f32[392,128]{1,0:T(8,128)S(1)} %get-tuple-element.128), channel_id=1, source_target_pairs={{0,15},{1,2},{2,1},{3,4},{4,3},{5,6},{6,5},{7,8},{8,7},{9,10},{10,... | collective-permute-start | bytes 602120 | tf_op jit(solution)/shard_map/ppermute | solution.py:56
  118.3 4.0 %collective-permute-done.18.refs_8_.refs_2_ = f32[192,128]{1,0:T(8,128)S(1)} collective-permute-done((f32[192,128]{1,0:T(8,128)S(1)}, f32[192,128]{1,0:T(8,128)S(1)}, u32[]{:S(2)}, u32[]{:S(2)}) %collective-permute-start.18) | collective-permute-done | bytes 98336 | tf_op jit(solution)/shard_map/ppermute | solution.py:56
  127.2 5.1 %collective-permute-start.21 = (f32[392,128]{1,0:T(8,128)S(1)}, f32[392,128]{1,0:T(8,128)S(1)}, u32[]{:S(2)}, u32[]{:S(2)}) collective-permute-start(f32[392,128]{1,0:T(8,128)S(1)} %get-tuple-element.135), channel_id=1, source_target_pairs={{0,15},{1,2},{2,1},{3,4},{4,3},{5,6},{6,5},{7,8},{8,7},{9,10},{10,... | collective-permute-start | bytes 602120 | tf_op jit(solution)/shard_map/ppermute | solution.py:56
  132.8 3.8 %shard_map.86.earlier.acc = f32[1536,128]{1,0:T(8,128)S(1)} custom-call(s32[6]{0:T(128)S(1)} %stack.52.info, f32[1536,128]{1,0:T(8,128)S(1)} %get-tuple-element.133.a_ref, f32[7680,128]{1,0:T(8,128)S(1)} %bitcast.29, f32[1536,128]{1,0:T(8,128)S(1)} %shard_map.83.earlier.acc, f32[392,128]{1,0:T(8,128)S(1)} %collective-permute-done.16.refs_6_.refs_0_, ...), custom_call_target="tpu_custom_call" | custom-call | flops 4000000 | bytes 5000000 | tf_op jit(solution)/shard_map/pallas_call | solution.py:549
  141.8 4.6 %collective-permute-start.25 = (f32[392,128]{1,0:T(8,128)S(1)}, f32[392,128]{1,0:T(8,128)S(1)}, u32[]{:S(2)}, u32[]{:S(2)}) collective-permute-start(f32[392,128]{1,0:T(8,128)S(1)} %get-tuple-element.141), channel_id=1, source_target_pairs={{0,15},{1,2},{2,1},{3,4},{4,3},{5,6},{6,5},{7,8},{8,7},{9,10},{10,... | collective-permute-start | bytes 602120 | tf_op jit(solution)/shard_map/ppermute | solution.py:56
  147.0 4.0 %collective-permute-done.26.refs_8_.refs_2_ = f32[192,128]{1,0:T(8,128)S(1)} collective-permute-done((f32[192,128]{1,0:T(8,128)S(1)}, f32[192,128]{1,0:T(8,128)S(1)}, u32[]{:S(2)}, u32[]{:S(2)}) %collective-permute-start.26) | collective-permute-done | bytes 98336 | tf_op jit(solution)/shard_map/ppermute | solution.py:56
  155.9 5.1 %collective-permute-start.29 = (f32[392,128]{1,0:T(8,128)S(1)}, f32[392,128]{1,0:T(8,128)S(1)}, u32[]{:S(2)}, u32[]{:S(2)}) collective-permute-start(f32[392,128]{1,0:T(8,128)S(1)} %get-tuple-element.148), channel_id=1, source_target_pairs={{0,15},{1,2},{2,1},{3,4},{4,3},{5,6},{6,5},{7,8},{8,7},{9,10},{10,... | collective-permute-start | bytes 602120 | tf_op jit(solution)/shard_map/ppermute | solution.py:56
  161.5 3.8 %shard_map.89.earlier.acc = f32[1536,128]{1,0:T(8,128)S(1)} custom-call(s32[6]{0:T(128)S(1)} %stack.52.info, f32[1536,128]{1,0:T(8,128)S(1)} %get-tuple-element.146.a_ref, f32[7680,128]{1,0:T(8,128)S(1)} %bitcast.31, f32[1536,128]{1,0:T(8,128)S(1)} %shard_map.86.earlier.acc, f32[392,128]{1,0:T(8,128)S(1)} %collective-permute-done.24.refs_6_.refs_0_, ...), custom_call_target="tpu_custom_call" | custom-call | flops 4000000 | bytes 5000000 | tf_op jit(solution)/shard_map/pallas_call | solution.py:549
  170.5 4.6 %collective-permute-start.33 = (f32[392,128]{1,0:T(8,128)S(1)}, f32[392,128]{1,0:T(8,128)S(1)}, u32[]{:S(2)}, u32[]{:S(2)}) collective-permute-start(f32[392,128]{1,0:T(8,128)S(1)} %get-tuple-element.154), channel_id=1, source_target_pairs={{0,15},{1,2},{2,1},{3,4},{4,3},{5,6},{6,5},{7,8},{8,7},{9,10},{10,... | collective-permute-start | bytes 602120 | tf_op jit(solution)/shard_map/ppermute | solution.py:56
  175.6 4.1 %collective-permute-done.34.refs_8_.refs_2_ = f32[192,128]{1,0:T(8,128)S(1)} collective-permute-done((f32[192,128]{1,0:T(8,128)S(1)}, f32[192,128]{1,0:T(8,128)S(1)}, u32[]{:S(2)}, u32[]{:S(2)}) %collective-permute-start.34) | collective-permute-done | bytes 98336 | tf_op jit(solution)/shard_map/ppermute | solution.py:56
  184.6 5.1 %collective-permute-start.37 = (f32[392,128]{1,0:T(8,128)S(1)}, f32[392,128]{1,0:T(8,128)S(1)}, u32[]{:S(2)}, u32[]{:S(2)}) collective-permute-start(f32[392,128]{1,0:T(8,128)S(1)} %get-tuple-element.161), channel_id=1, source_target_pairs={{0,15},{1,2},{2,1},{3,4},{4,3},{5,6},{6,5},{7,8},{8,7},{9,10},{10,... | collective-permute-start | bytes 602120 | tf_op jit(solution)/shard_map/ppermute | solution.py:56
  199.4 4.6 %collective-permute-start.41 = (f32[200,128]{1,0:T(8,128)S(1)}, f32[200,128]{1,0:T(8,128)S(1)}, u32[]{:S(2)}, u32[]{:S(2)}) collective-permute-start(f32[200,128]{1,0:T(8,128)S(1)} %get-tuple-element.166), channel_id=1, source_target_pairs={{0,15},{1,2},{2,1},{3,4},{4,3},{5,6},{6,5},{7,8},{8,7},{9,10},{10,... | collective-permute-start | bytes 307208 | tf_op jit(solution)/shard_map/ppermute | solution.py:56
  210.2 3.9 %shard_map.94.acc = f32[1536,128]{1,0:T(8,128)S(1)} custom-call(s32[6]{0:T(128)S(1)} %stack.52.info, f32[1536,128]{1,0:T(8,128)S(1)} %get-tuple-element.164.a_ref, f32[7680,128]{1,0:T(8,128)S(1)} %bitcast.34, f32[1536,128]{1,0:T(8,128)S(1)} %shard_map.92.earlier.acc, f32[200,128]{1,0:T(8,128)S(1)} %collective-permute-done.40.refs_0_.rxa, ...), custom_call_target="tpu_custom_call" | custom-call | flops 4000000 | bytes 5000000 | tf_op jit(solution)/shard_map/pallas_call | solution.py:549
  215.9 10.0 %all_to_all.5 = f32[8,72,32]{1,2,0:T(8,128)S(1)} all-to-all(f32[8,72,32]{1,2,0:T(8,128)S(1)} %copy.8), channel_id=1, replica_groups=mesh['depth'=8,'strip'=16] {'depth'}, dimensions={0} | all-to-all | bytes 147456 | tf_op jit(solution)/shard_map/all_to_all | solution.py:567
  227.7 6.7 %collective-permute-done.45.rb = f32[128,128]{1,0:T(8,128)S(1)} collective-permute-done((f32[128,128]{1,0:T(8,128)S(1)}, f32[128,128]{1,0:T(8,128)S(1)}, u32[]{:S(2)}, u32[]{:S(2)}) %collective-permute-start.45) | collective-permute-done | bytes 65568 | tf_op jit(solution)/shard_map/ppermute | solution.py:56
  236.7 6.4 %collective-permute-done.47.rb = f32[192,128]{1,0:T(8,128)S(1)} collective-permute-done((f32[192,128]{1,0:T(8,128)S(1)}, f32[192,128]{1,0:T(8,128)S(1)}, u32[]{:S(2)}, u32[]{:S(2)}) %collective-permute-start.47) | collective-permute-done | bytes 98336 | tf_op jit(solution)/shard_map/ppermute | solution.py:56
  245.2 5.8 %collective-permute-done.49.rb = f32[64,128]{1,0:T(8,128)S(1)} collective-permute-done((f32[64,128]{1,0:T(8,128)S(1)}, f32[64,128]{1,0:T(8,128)S(1)}, u32[]{:S(2)}, u32[]{:S(2)}) %collective-permute-start.49) | collective-permute-done | bytes 32800 | tf_op jit(solution)/shard_map/ppermute | solution.py:56
  (198 shorter events, 122.5 us)
Async XLA Ops:
  21.4 10.1 %collective-permute-start = (f32[672,128]{1,0:T(8,128)S(1)}, f32[672,128]{1,0:T(8,128)S(1)}, u32[]{:S(2)}, u32[]{:S(2)}) collective-permute-start(f32[672,128]{1,0:T(8,128)S(1)} %get-tuple-element.96), channel_id=1, source_target_pairs={{0,1},{1,0},{2,3},{3,2},{4,5},{5,4},{6,7},{7,6},{8,9},{9,8},{10,11... | collective-permute-start | bytes 1032200 | tf_op jit(solution)/shard_map/ppermute | solution.py:56
  21.4 10.6 %collective-permute-start.1 = (f32[672,128]{1,0:T(8,128)S(1)}, f32[672,128]{1,0:T(8,128)S(1)}, u32[]{:S(2)}, u32[]{:S(2)}) collective-permute-start(f32[672,128]{1,0:T(8,128)S(1)} %get-tuple-element.97), channel_id=1, source_target_pairs={{0,15},{1,2},{2,1},{3,4},{4,3},{5,6},{6,5},{7,8},{8,7},{9,10},{10,... | collective-permute-start | bytes 1032200 | tf_op jit(solution)/shard_map/ppermute | solution.py:56
  28.9 8.4 %collective-permute-start.3 = (f32[192,128]{1,0:T(8,128)S(1)}, f32[192,128]{1,0:T(8,128)S(1)}, u32[]{:S(2)}, u32[]{:S(2)}) collective-permute-start(f32[192,128]{1,0:T(8,128)S(1)} %get-tuple-element.99), channel_id=1, source_target_pairs={{0,112},{16,32},{32,16},{48,64},{64,48},{80,96},{96,80},{112,0},{1... | collective-permute-start | bytes 294920 | tf_op jit(solution)/shard_map/ppermute | solution.py:56
  59.5 15.2 %collective-permute-start.6 = (f32[392,128]{1,0:T(8,128)}, f32[392,128]{1,0:T(8,128)}, u32[]{:S(2)}, u32[]{:S(2)}) collective-permute-start(f32[392,128]{1,0:T(8,128)} %get-tuple-element.111), channel_id=1, source_target_pairs={{0,1},{1,0},{2,3},{3,2},{4,5},{5,4},{6,7},{7,6},{8,9},{9,8},{10,11... | collective-permute-start | bytes 602120 | tf_op jit(solution)/shard_map/ppermute | solution.py:56
  61.2 13.4 %collective-permute-start.7 = (f32[392,128]{1,0:T(8,128)}, f32[392,128]{1,0:T(8,128)}, u32[]{:S(2)}, u32[]{:S(2)}) collective-permute-start(f32[392,128]{1,0:T(8,128)} %get-tuple-element.112), channel_id=1, source_target_pairs={{0,15},{1,2},{2,1},{3,4},{4,3},{5,6},{6,5},{7,8},{8,7},{9,10},{10,... | collective-permute-start | bytes 602120 | tf_op jit(solution)/shard_map/ppermute | solution.py:56
  65.6 9.0 %collective-permute-start.5 = (f32[336,128]{1,0:T(8,128)}, f32[336,128]{1,0:T(8,128)}, u32[]{:S(2)}, u32[]{:S(2)}) collective-permute-start(f32[336,128]{1,0:T(8,128)} %get-tuple-element.107), channel_id=1, source_target_pairs={{0,112},{16,32},{32,16},{48,64},{64,48},{80,96},{96,80},{112,0},{1... | collective-permute-start | bytes 516104 | tf_op jit(solution)/shard_map/ppermute | solution.py:56
  84.2 12.0 %collective-permute-start.8 = (f32[392,128]{1,0:T(8,128)S(1)}, f32[392,128]{1,0:T(8,128)S(1)}, u32[]{:S(2)}, u32[]{:S(2)}) collective-permute-start(f32[392,128]{1,0:T(8,128)S(1)} %get-tuple-element.114), channel_id=1, source_target_pairs={{0,1},{1,0},{2,3},{3,2},{4,5},{5,4},{6,7},{7,6},{8,9},{9,8},{10,11... | collective-permute-start | bytes 602120 | tf_op jit(solution)/shard_map/ppermute | solution.py:56
  84.2 12.0 %collective-permute-start.9 = (f32[392,128]{1,0:T(8,128)S(1)}, f32[392,128]{1,0:T(8,128)S(1)}, u32[]{:S(2)}, u32[]{:S(2)}) collective-permute-start(f32[392,128]{1,0:T(8,128)S(1)} %get-tuple-element.115), channel_id=1, source_target_pairs={{0,15},{1,2},{2,1},{3,4},{4,3},{5,6},{6,5},{7,8},{8,7},{9,10},{10,... | collective-permute-start | bytes 602120 | tf_op jit(solution)/shard_map/ppermute | solution.py:56
  98.9 11.4 %collective-permute-start.12 = (f32[392,128]{1,0:T(8,128)S(1)}, f32[392,128]{1,0:T(8,128)S(1)}, u32[]{:S(2)}, u32[]{:S(2)}) collective-permute-start(f32[392,128]{1,0:T(8,128)S(1)} %get-tuple-element.121), channel_id=1, source_target_pairs={{0,1},{1,0},{2,3},{3,2},{4,5},{5,4},{6,7},{7,6},{8,9},{9,8},{10,11... | collective-permute-start | bytes 602120 | tf_op jit(solution)/shard_map/ppermute | solution.py:56
  99.0 11.3 %collective-permute-start.13 = (f32[392,128]{1,0:T(8,128)S(1)}, f32[392,128]{1,0:T(8,128)S(1)}, u32[]{:S(2)}, u32[]{:S(2)}) collective-permute-start(f32[392,128]{1,0:T(8,128)S(1)} %get-tuple-element.122), channel_id=1, source_target_pairs={{0,15},{1,2},{2,1},{3,4},{4,3},{5,6},{6,5},{7,8},{8,7},{9,10},{10,... | collective-permute-start | bytes 602120 | tf_op jit(solution)/shard_map/ppermute | solution.py:56
  113.0 11.4 %collective-permute-start.16 = (f32[392,128]{1,0:T(8,128)S(1)}, f32[392,128]{1,0:T(8,128)S(1)}, u32[]{:S(2)}, u32[]{:S(2)}) collective-permute-start(f32[392,128]{1,0:T(8,128)S(1)} %get-tuple-element.127), channel_id=1, source_target_pairs={{0,1},{1,0},{2,3},{3,2},{4,5},{5,4},{6,7},{7,6},{8,9},{9,8},{10,11... | collective-permute-start | bytes 602120 | tf_op jit(solution)/shard_map/ppermute | solution.py:56
  113.1 11.3 %collective-permute-start.17 = (f32[392,128]{1,0:T(8,128)S(1)}, f32[392,128]{1,0:T(8,128)S(1)}, u32[]{:S(2)}, u32[]{:S(2)}) collective-permute-start(f32[392,128]{1,0:T(8,128)S(1)} %get-tuple-element.128), channel_id=1, source_target_pairs={{0,15},{1,2},{2,1},{3,4},{4,3},{5,6},{6,5},{7,8},{8,7},{9,10},{10,... | collective-permute-start | bytes 602120 | tf_op jit(solution)/shard_map/ppermute | solution.py:56
  127.1 11.9 %collective-permute-start.20 = (f32[392,128]{1,0:T(8,128)S(1)}, f32[392,128]{1,0:T(8,128)S(1)}, u32[]{:S(2)}, u32[]{:S(2)}) collective-permute-start(f32[392,128]{1,0:T(8,128)S(1)} %get-tuple-element.134), channel_id=1, source_target_pairs={{0,1},{1,0},{2,3},{3,2},{4,5},{5,4},{6,7},{7,6},{8,9},{9,8},{10,11... | collective-permute-start | bytes 602120 | tf_op jit(solution)/shard_map/ppermute | solution.py:56
  127.2 11.8 %collective-permute-start.21 = (f32[392,128]{1,0:T(8,128)S(1)}, f32[392,128]{1,0:T(8,128)S(1)}, u32[]{:S(2)}, u32[]{:S(2)}) collective-permute-start(f32[392,128]{1,0:T(8,128)S(1)} %get-tuple-element.135), channel_id=1, source_target_pairs={{0,15},{1,2},{2,1},{3,4},{4,3},{5,6},{6,5},{7,8},{8,7},{9,10},{10,... | collective-permute-start | bytes 602120 | tf_op jit(solution)/shard_map/ppermute | solution.py:56
  141.7 11.4 %collective-permute-start.24 = (f32[392,128]{1,0:T(8,128)S(1)}, f32[392,128]{1,0:T(8,128)S(1)}, u32[]{:S(2)}, u32[]{:S(2)}) collective-permute-start(f32[392,128]{1,0:T(8,128)S(1)} %get-tuple-element.140), channel_id=1, source_target_pairs={{0,1},{1,0},{2,3},{3,2},{4,5},{5,4},{6,7},{7,6},{8,9},{9,8},{10,11... | collective-permute-start | bytes 602120 | tf_op jit(solution)/shard_map/ppermute | solution.py:56
  141.8 11.3 %collective-permute-start.25 = (f32[392,128]{1,0:T(8,128)S(1)}, f32[392,128]{1,0:T(8,128)S(1)}, u32[]{:S(2)}, u32[]{:S(2)}) collective-permute-start(f32[392,128]{1,0:T(8,128)S(1)} %get-tuple-element.141), channel_id=1, source_target_pairs={{0,15},{1,2},{2,1},{3,4},{4,3},{5,6},{6,5},{7,8},{8,7},{9,10},{10,... | collective-permute-start | bytes 602120 | tf_op jit(solution)/shard_map/ppermute | solution.py:56
  155.8 11.9 %collective-permute-start.28 = (f32[392,128]{1,0:T(8,128)S(1)}, f32[392,128]{1,0:T(8,128)S(1)}, u32[]{:S(2)}, u32[]{:S(2)}) collective-permute-start(f32[392,128]{1,0:T(8,128)S(1)} %get-tuple-element.147), channel_id=1, source_target_pairs={{0,1},{1,0},{2,3},{3,2},{4,5},{5,4},{6,7},{7,6},{8,9},{9,8},{10,11... | collective-permute-start | bytes 602120 | tf_op jit(solution)/shard_map/ppermute | solution.py:56
  155.9 11.8 %collective-permute-start.29 = (f32[392,128]{1,0:T(8,128)S(1)}, f32[392,128]{1,0:T(8,128)S(1)}, u32[]{:S(2)}, u32[]{:S(2)}) collective-permute-start(f32[392,128]{1,0:T(8,128)S(1)} %get-tuple-element.148), channel_id=1, source_target_pairs={{0,15},{1,2},{2,1},{3,4},{4,3},{5,6},{6,5},{7,8},{8,7},{9,10},{10,... | collective-permute-start | bytes 602120 | tf_op jit(solution)/shard_map/ppermute | solution.py:56
  170.4 11.4 %collective-permute-start.32 = (f32[392,128]{1,0:T(8,128)S(1)}, f32[392,128]{1,0:T(8,128)S(1)}, u32[]{:S(2)}, u32[]{:S(2)}) collective-permute-start(f32[392,128]{1,0:T(8,128)S(1)} %get-tuple-element.153), channel_id=1, source_target_pairs={{0,1},{1,0},{2,3},{3,2},{4,5},{5,4},{6,7},{7,6},{8,9},{9,8},{10,11... | collective-permute-start | bytes 602120 | tf_op jit(solution)/shard_map/ppermute | solution.py:56
  170.5 11.3 %collective-permute-start.33 = (f32[392,128]{1,0:T(8,128)S(1)}, f32[392,128]{1,0:T(8,128)S(1)}, u32[]{:S(2)}, u32[]{:S(2)}) collective-permute-start(f32[392,128]{1,0:T(8,128)S(1)} %get-tuple-element.154), channel_id=1, source_target_pairs={{0,15},{1,2},{2,1},{3,4},{4,3},{5,6},{6,5},{7,8},{8,7},{9,10},{10,... | collective-permute-start | bytes 602120 | tf_op jit(solution)/shard_map/ppermute | solution.py:56
  184.5 11.9 %collective-permute-start.36 = (f32[392,128]{1,0:T(8,128)S(1)}, f32[392,128]{1,0:T(8,128)S(1)}, u32[]{:S(2)}, u32[]{:S(2)}) collective-permute-start(f32[392,128]{1,0:T(8,128)S(1)} %get-tuple-element.160), channel_id=1, source_target_pairs={{0,1},{1,0},{2,3},{3,2},{4,5},{5,4},{6,7},{7,6},{8,9},{9,8},{10,11... | collective-permute-start | bytes 602120 | tf_op jit(solution)/shard_map/ppermute | solution.py:56
  184.6 11.8 %collective-permute-start.37 = (f32[392,128]{1,0:T(8,128)S(1)}, f32[392,128]{1,0:T(8,128)S(1)}, u32[]{:S(2)}, u32[]{:S(2)}) collective-permute-start(f32[392,128]{1,0:T(8,128)S(1)} %get-tuple-element.161), channel_id=1, source_target_pairs={{0,15},{1,2},{2,1},{3,4},{4,3},{5,6},{6,5},{7,8},{8,7},{9,10},{10,... | collective-permute-start | bytes 602120 | tf_op jit(solution)/shard_map/ppermute | solution.py:56
  199.4 10.8 %collective-permute-start.40 = (f32[200,128]{1,0:T(8,128)S(1)}, f32[200,128]{1,0:T(8,128)S(1)}, u32[]{:S(2)}, u32[]{:S(2)}) collective-permute-start(f32[200,128]{1,0:T(8,128)S(1)} %get-tuple-element.165), channel_id=1, source_target_pairs={{0,1},{1,0},{2,3},{3,2},{4,5},{5,4},{6,7},{7,6},{8,9},{9,8},{10,11... | collective-permute-start | bytes 307208 | tf_op jit(solution)/shard_map/ppermute | solution.py:56
  199.4 10.8 %collective-permute-start.41 = (f32[200,128]{1,0:T(8,128)S(1)}, f32[200,128]{1,0:T(8,128)S(1)}, u32[]{:S(2)}, u32[]{:S(2)}) collective-permute-start(f32[200,128]{1,0:T(8,128)S(1)} %get-tuple-element.166), channel_id=1, source_target_pairs={{0,15},{1,2},{2,1},{3,4},{4,3},{5,6},{6,5},{7,8},{8,7},{9,10},{10,... | collective-permute-start | bytes 307208 | tf_op jit(solution)/shard_map/ppermute | solution.py:56
  (70 other events, 398.4 us)
